TPU v7x, 32 devices: a whole 2x2x4 slice. The times are simulated.
32 devices in a mesh: cube: 8 (over y, x, core), spec: 4 (over z).
Axes of the slice: x: 2, y: 2, z: 4, core: 2. Of those that a mesh axis runs over, the one named last changes fastest.
Arguments:
- tokens: bfloat16 [8, 1536, 768], P('cube', 'spec'), may hold values from -6 to 6
- cotangent: bfloat16 [8, 1536, 768], P('cube', 'spec'), may hold values from -24 to 24
- lengths: int32 [8], P('cube'), may hold values from 864 to 1536, as said below
- projection: bfloat16 [768, 2304], replicated, may hold values from -0.21875 to 0.21875
- query_bias: float32 [768], replicated, may hold values from -3 to 3
- value_bias: float32 [768], replicated, may hold values from -3 to 3
- output_weight: bfloat16 [768, 768], replicated, may hold values from -0.21875 to 0.21875
- output_bias: float32 [768], replicated, may hold values from -3 to 3
- up_weight: bfloat16 [768, 3072], replicated, may hold values from -0.21875 to 0.21875
- up_bias: float32 [3072], replicated, may hold values from -3 to 3
- down_weight: bfloat16 [3072, 768], replicated, may hold values from -0.109375 to 0.109375
- down_bias: float32 [768], replicated, may hold values from -3 to 3
- first_gain: float32 [768], replicated, may hold values from 0.1 to 1.9
- first_shift: float32 [768], replicated, may hold values from -3 to 3
- second_gain: float32 [768], replicated, may hold values from 0.1 to 1.9
- second_shift: float32 [768], replicated, may hold values from -3 to 3
Outputs:
- block_out: bfloat16 [8, 1536, 768], P('cube', 'spec')
- grad_tokens: float32 [8, 1536, 768], P('cube', 'spec')
- grad_projection: float32 [768, 2304], P('cube', 'spec')
- grad_query_bias: float32 [768], replicated
- grad_value_bias: float32 [768], replicated
- grad_output_weight: float32 [768, 768], P('cube', 'spec')
- grad_output_bias: float32 [768], replicated
- grad_up_weight: float32 [768, 3072], P('cube', 'spec')
- grad_up_bias: float32 [3072], replicated
- grad_down_weight: float32 [3072, 768], P('cube', 'spec')
- grad_down_bias: float32 [768], replicated
- grad_first_gain: float32 [768], replicated
- grad_first_shift: float32 [768], replicated
- grad_second_gain: float32 [768], replicated
- grad_second_shift: float32 [768], replicated
Inputs may be any that keep to these rules, and one draw needn't show every extreme that they name: `lengths`: each cube's length is 1536 or 864, and both occur.
All inputs are finite; a program needn't handle non-finite values.
Results may differ from a plain program's by a relative error of at most 0.012.
Values may be sent and summed in bfloat16 or wider, within the bound.
No kernel may reach another device: no remote copies, remote signals or barrier semaphores. Data moves between devices by JAX's collectives and lax.ppermute only.
A program may use at most 192 MiB of HBM per device.

v0:
```python
from functools import partial

import jax
import jax.numpy as jnp
from jax import lax
from jax.sharding import PartitionSpec as P

HEADS = 12
HD = 64


EPS = 1e-06


def normalize(values):
    average = jnp.mean(values, -1, keepdims=True)
    centred = values - average
    inverse = lax.rsqrt(jnp.mean(centred * centred, -1, keepdims=True) + EPS)
    return (centred * inverse, inverse)


def norm_back(grad_out, normed, inverse, gain):
    grad_gain = jnp.sum(grad_out * normed, 0)
    grad_shift = jnp.sum(grad_out, 0)
    scaled = grad_out * gain
    grad_in = inverse * (
        scaled
        - jnp.mean(scaled, -1, keepdims=True)
        - normed * jnp.mean(scaled * normed, -1, keepdims=True)
    )
    return (grad_in, grad_gain, grad_shift)


def left_dot(left, right):
    return lax.dot_general(
        left, right, (((0,), (0,)), ((), ())), preferred_element_type=jnp.float32
    )


def right_dot(left, right):
    return lax.dot_general(
        left, right, (((1,), (1,)), ((), ())), preferred_element_type=jnp.float32
    )


def scores_of(queries, all_keys, key_mask):
    scores = jnp.einsum(
        "qhd,khd->hqk",
        queries.reshape(queries.shape[0], HEADS, HD),
        all_keys.reshape(all_keys.shape[0], HEADS, HD),
        preferred_element_type=jnp.float32,
    ) * HD ** (-0.5)
    return jnp.where(key_mask[None, None, :], scores, -1e30)


def attend(members):
    queries, all_keys, values, key_mask = members
    scores = scores_of(queries, all_keys, key_mask)
    row_top = jnp.max(scores, -1, keepdims=True)
    log_total = jnp.log(jnp.sum(jnp.exp(scores - row_top), -1, keepdims=True)) + row_top
    weights = jnp.exp(scores - log_total).astype(jnp.bfloat16)
    attended = jnp.einsum(
        "hqk,khd->qhd",
        weights,
        values.reshape(values.shape[0], HEADS, HD),
        preferred_element_type=jnp.float32,
    )
    return (attended.reshape(queries.shape[0], -1), log_total)


def attend_back(members):
    queries, all_keys, values, key_mask, log_total, grad_attended = members
    row_count = queries.shape[0]
    key_count = all_keys.shape[0]
    softmaxed = jnp.exp(scores_of(queries, all_keys, key_mask) - log_total)
    grad_heads = grad_attended.reshape(row_count, HEADS, HD)
    key_heads = all_keys.reshape(key_count, HEADS, HD)
    grad_weights = jnp.einsum(
        "qhd,khd->hqk",
        grad_heads,
        values.reshape(key_count, HEADS, HD),
        preferred_element_type=jnp.float32,
    )
    spread = jnp.sum(softmaxed * grad_weights, -1, keepdims=True)
    grad_scores = (softmaxed * (grad_weights - spread)).astype(jnp.bfloat16)
    factor = HD ** (-0.5)
    grad_queries = factor * jnp.einsum(
        "hqk,khd->qhd", grad_scores, key_heads, preferred_element_type=jnp.float32
    )
    grad_keys = factor * jnp.einsum(
        "hqk,qhd->khd",
        grad_scores,
        queries.reshape(row_count, HEADS, HD),
        preferred_element_type=jnp.float32,
    )
    grad_values = jnp.einsum(
        "hqk,qhd->khd",
        softmaxed.astype(jnp.bfloat16),
        grad_heads,
        preferred_element_type=jnp.float32,
    )
    return (
        grad_queries.reshape(row_count, -1),
        grad_keys.reshape(key_count, -1),
        grad_values.reshape(key_count, -1),
    )


def local(
    tokens,
    cotangent,
    lengths,
    projection,
    query_bias,
    value_bias,
    output_weight,
    output_bias,
    up_weight,
    up_bias,
    down_weight,
    down_bias,
    first_gain,
    first_shift,
    second_gain,
    second_shift,
):
    cube_count, row_count, model_width = tokens.shape
    total_rows = row_count * lax.axis_size("spec")
    flat_rows = cube_count * row_count
    inputs = tokens.reshape(flat_rows, model_width).astype(jnp.float32)
    normed_one, inverse_one = normalize(inputs)
    hidden_one = (normed_one * first_gain + first_shift).astype(jnp.bfloat16)
    projected = jnp.dot(hidden_one, projection, preferred_element_type=jnp.float32)
    queries = (
        (projected[:, :model_width] + query_bias)
        .astype(jnp.bfloat16)
        .reshape(cube_count, row_count, model_width)
    )
    key_part = (
        projected[:, model_width : 2 * model_width]
        .astype(jnp.bfloat16)
        .reshape(cube_count, row_count, model_width)
    )
    value_part = (
        (projected[:, 2 * model_width :] + value_bias)
        .astype(jnp.bfloat16)
        .reshape(cube_count, row_count, model_width)
    )
    all_keys, values = (
        lax.all_gather(key_part, "spec", axis=1, tiled=True),
        lax.all_gather(value_part, "spec", axis=1, tiled=True),
    )
    key_mask = jnp.arange(total_rows)[None, :] < lengths[:, None]
    attended, log_total = lax.map(attend, (queries, all_keys, values, key_mask))
    attended = attended.reshape(flat_rows, model_width).astype(jnp.bfloat16)
    middle = inputs + (
        jnp.dot(attended, output_weight, preferred_element_type=jnp.float32) + output_bias
    )
    normed_two, inverse_two = normalize(middle)
    hidden_two = (normed_two * second_gain + second_shift).astype(jnp.bfloat16)
    before = jnp.dot(hidden_two, up_weight, preferred_element_type=jnp.float32) + up_bias
    gelu_exact = partial(jax.nn.gelu, approximate=False)
    lifted = gelu_exact(before).astype(jnp.bfloat16)
    result = middle + (jnp.dot(lifted, down_weight, preferred_element_type=jnp.float32) + down_bias)
    block_out = result.astype(jnp.bfloat16).reshape(cube_count, row_count, model_width)
    grad_out = cotangent.reshape(flat_rows, model_width)
    grad_down_weight = left_dot(lifted, grad_out)
    grad_down_bias = jnp.sum(grad_out.astype(jnp.float32), 0)
    grad_lifted = right_dot(grad_out, down_weight)
    grad_before = jax.vjp(gelu_exact, before)[1](grad_lifted)[0].astype(jnp.bfloat16)
    grad_up_weight = left_dot(hidden_two, grad_before)
    grad_up_bias = jnp.sum(grad_before.astype(jnp.float32), 0)
    grad_hidden_two = right_dot(grad_before, up_weight)
    grad_norm_two, grad_second_gain, grad_second_shift = norm_back(
        grad_hidden_two, normed_two, inverse_two, second_gain
    )
    grad_middle = grad_out.astype(jnp.float32) + grad_norm_two
    grad_branch = grad_middle.astype(jnp.bfloat16)
    grad_output_weight = left_dot(attended, grad_branch)
    grad_output_bias = jnp.sum(grad_branch.astype(jnp.float32), 0)
    grad_attended = (
        right_dot(grad_branch, output_weight)
        .astype(jnp.bfloat16)
        .reshape(cube_count, row_count, model_width)
    )
    keys_back, values_back = (all_keys, values)
    grad_queries, grad_keys, grad_values = lax.map(
        attend_back, (queries, keys_back, values_back, key_mask, log_total, grad_attended)
    )
    grad_keys, grad_values = (
        lax.psum_scatter(
            grad_keys.astype(jnp.bfloat16), "spec", scatter_dimension=1, tiled=True
        ).astype(jnp.float32),
        lax.psum_scatter(
            grad_values.astype(jnp.bfloat16), "spec", scatter_dimension=1, tiled=True
        ).astype(jnp.float32),
    )
    grad_joined = jnp.concatenate(
        [
            grad_queries.astype(jnp.bfloat16),
            grad_keys.astype(jnp.bfloat16),
            grad_values.astype(jnp.bfloat16),
        ],
        -1,
    ).reshape(flat_rows, 3 * model_width)
    grad_projection = left_dot(hidden_one, grad_joined)
    grad_query_bias = jnp.sum(grad_joined[:, :model_width].astype(jnp.float32), 0)
    grad_value_bias = jnp.sum(grad_joined[:, 2 * model_width :].astype(jnp.float32), 0)
    grad_hidden_one = right_dot(grad_joined, projection)
    grad_norm_one, grad_first_gain, grad_first_shift = norm_back(
        grad_hidden_one, normed_one, inverse_one, first_gain
    )
    grad_tokens = (grad_middle + grad_norm_one).reshape(cube_count, row_count, model_width)
    vector_total = lax.psum(
        (
            grad_query_bias,
            grad_value_bias,
            grad_output_bias,
            grad_up_bias,
            grad_down_bias,
            grad_first_gain,
            grad_first_shift,
            grad_second_gain,
            grad_second_shift,
        ),
        ("cube", "spec"),
    )
    matrices = (grad_projection, grad_output_weight, grad_up_weight, grad_down_weight)
    matrices = (
        lax.psum_scatter(matrices[0], "cube", scatter_dimension=0, tiled=True),
        lax.psum_scatter(matrices[1], "cube", scatter_dimension=0, tiled=True),
        lax.psum_scatter(matrices[2], "cube", scatter_dimension=0, tiled=True),
        lax.psum_scatter(matrices[3], "cube", scatter_dimension=0, tiled=True),
    )
    matrices = (
        lax.psum_scatter(
            matrices[0].astype(jnp.bfloat16), "spec", scatter_dimension=1, tiled=True
        ).astype(jnp.float32),
        lax.psum_scatter(
            matrices[1].astype(jnp.bfloat16), "spec", scatter_dimension=1, tiled=True
        ).astype(jnp.float32),
        lax.psum_scatter(
            matrices[2].astype(jnp.bfloat16), "spec", scatter_dimension=1, tiled=True
        ).astype(jnp.float32),
        lax.psum_scatter(
            matrices[3].astype(jnp.bfloat16), "spec", scatter_dimension=1, tiled=True
        ).astype(jnp.float32),
    )
    return (
        block_out,
        grad_tokens,
        matrices[0],
        vector_total[0],
        vector_total[1],
        matrices[1],
        vector_total[2],
        matrices[2],
        vector_total[3],
        matrices[3],
        vector_total[4],
        vector_total[5],
        vector_total[6],
        vector_total[7],
        vector_total[8],
    )


def solution(mesh):
    return jax.shard_map(
        local,
        mesh=mesh,
        in_specs=(
            P("cube", "spec", None),
            P("cube", "spec", None),
            P("cube"),
            P(),
            P(),
            P(),
            P(),
            P(),
            P(),
            P(),
            P(),
            P(),
            P(),
            P(),
            P(),
            P(),
        ),
        out_specs=(
            P("cube", "spec", None),
            P("cube", "spec", None),
            P("cube", "spec"),
            P(),
            P(),
            P("cube", "spec"),
            P(),
            P("cube", "spec"),
            P(),
            P("cube", "spec"),
            P(),
            P(),
            P(),
            P(),
            P(),
        ),
        check_vma=False,
    )
```

profile of v0, /device:TPU:0, one launch (start us, length us, event | category | flops | bytes accessed | tf_op | source)
XLA Modules:
  0.0 653.1 jit_solution(8041948476160373560)
XLA Ops:
  21.2 47.6 %all-gather.7.cloned.1.call-done = bf16[1536,768]{1,0:T(8,128)(2,1)} async-done(((bf16[384,768]{1,0:T(8,128)(2,1)}), bf16[1536,768]{1,0:T(8,128)(2,1)}) %all-gather.7.cloned.1.call-update) | async-done | bytes 2359312 | tf_op jit(solution)/shard_map/all_gather | solution.py:150
  68.8 4.3 copy.47
  73.1 15.3 %fusion = (f32[12,384]{1,0:T(8,128)S(1)}, f32[12,384,1536]{2,1,0:T(8,128)}) fusion(pred[1536]{0:T(1024)(128)(4,1)S(1)} %iota_compare_fusion, bf16[384,12,64]{0,2,1:T(8,128)(2,1)} %bitcast.131, bf16[1536,12,64]{0,2,1:T(8,128)(2,1)} %bitcast.124), kind=kOutput, calls=%fused_computation.5 | convolution fusion | flops 927198720 | bytes 31280640 | tf_op jit(solution)/shard_map/while/body/eval_jaxpr/qhd,khd->hqk/dot_general | solution.py:47
  88.4 13.3 %exponential_reduce_fusion = f32[12,384]{1,0:T(8,128)S(1)} fusion(f32[12,384,1536]{2,1,0:T(8,128)} %get-tuple-element.138, f32[12,384]{1,0:T(8,128)S(1)} %get-tuple-element.137, pred[1536]{0:T(1024)(128)(4,1)S(1)} %iota_compare_fusion), kind=kLoop, calls=%fused_computation.3 | loop fusion | flops 28306944 | bytes 28349952 | tf_op jit(solution)/shard_map/while/body/eval_jaxpr/reduce_sum | solution.py:60
  102.3 18.0 %all-gather.5.cloned.1.call-done = bf16[1536,768]{1,0:T(8,128)(2,1)} async-done(((bf16[384,768]{1,0:T(8,128)(2,1)}), bf16[1536,768]{1,0:T(8,128)(2,1)}) %all-gather.5.cloned.1.call-update) | async-done | bytes 2359312 | tf_op jit(solution)/shard_map/all_gather | solution.py:151
  120.3 4.3 copy.45
  124.6 12.9 %convolution_convert_fusion.1 = bf16[12,64,384]{2,1,0:T(8,128)(2,1)S(1)} fusion(bf16[1536,12,64]{0,2,1:T(8,128)(2,1)} %bitcast.126, f32[12,384,1536]{2,1,0:T(8,128)} %get-tuple-element.138, f32[12,384]{1,0:T(8,128)} %log_add_fusion, pred[1536]{0:T(1024)(128)(4,1)S(1)} %iota_compare_fusion), kind=kOutput, calls=%fused_computation.48 | convolution fusion | flops 934576128 | bytes 31280640 | tf_op jit(solution)/shard_map/while/body/eval_jaxpr/hqk,khd->qhd/dot_general | solution.py:62
  138.7 16.3 %multiply_convert_fusion.2 = (bf16[384,3072]{1,0:T(8,128)(2,1)}, f32[384,3072]{1,0:T(8,128)S(1)}, f32[384,3072]{1,0:T(8,128)}) fusion(f32[3072]{0:T(1024)S(1)} %copy-done.28, bf16[768,3072]{1,0:T(8,128)(2,1)} %param.24, f32[384,768]{1,0:T(8,128)S(1)} %get-tuple-element.140, f32[768]{0:T(1024)S(1)} %copy-done.16, f32[768]{0:T(1024)S(1)} %copy-done.15, ...), kind=kOutput, calls=%fused_computation.12 | convolution fusion | flops 1891270656 | bytes 17716224 | tf_op jit(solution)/shard_map/dot_general | solution.py:161
  155.1 5.9 convert_reduce_fusion
  170.9 15.2 %convolution_convert_fusion = bf16[12,64,1536]{2,1,0:T(8,128)(2,1)} fusion(bf16[384,12,64]{0,2,1:T(8,128)(2,1)} %bitcast.138, f32[12,384,1536]{2,1,0:T(8,128)} %get-tuple-element.138, f32[12,384]{1,0:T(8,128)} %log_add_fusion, pred[1536]{0:T(1024)(128)(4,1)S(1)} %iota_compare_fusion), kind=kOutput, calls=%fused_computation.27 | convolution fusion | flops 935460864 | bytes 31280640 | tf_op jit(solution)/shard_map/while/body/eval_jaxpr/hqk,qhd->khd/dot_general | solution.py:96
  186.1 12.1 %copy.52 = bf16[1,1536,768]{2,0,1:T(2,128)(2,1)} copy(bf16[1,1536,768]{1,2,0:T(8,128)(2,1)} %bitcast.140) | data formatting | bytes 4718592
  198.2 4.4 copy.64
  202.7 23.5 %multiply_reduce_fusion = (f32[12,384]{1,0:T(8,128)}, f32[12,384,1536]{2,1,0:T(8,128)}) fusion(f32[12,384,1536]{2,1,0:T(8,128)} %get-tuple-element.138, f32[12,384]{1,0:T(8,128)S(1)} %copy-done.14, pred[1536]{0:T(1024)(128)(4,1)S(1)} %iota_compare_fusion, bf16[384,12,64]{0,2,1:T(8,128)(2,1)S(1)} %bitcast.139, bf16[1536,12,64]{0,2,1:T(8,128)(2,1)S(1)} %bitcast.127), kind=kOutput, calls=%fused_computation.1 | convolution fusion | flops 941354496 | bytes 59610624 | tf_op jit(solution)/shard_map/while/body/eval_jaxpr/qhd,khd->hqk/dot_general | solution.py:78
  226.2 24.1 %multiply_convert_fusion = bf16[12,384,1536]{2,1,0:T(8,128)(2,1)} fusion(f32[12,384,1536]{2,1,0:T(8,128)} %get-tuple-element.144, f32[12,384,1536]{2,1,0:T(8,128)} %get-tuple-element.138, f32[12,384]{1,0:T(8,128)} %get-tuple-element.143, f32[12,384]{1,0:T(8,128)} %log_add_fusion, pred[1536]{0:T(1024)(128)(4,1)S(1)} %iota_compare_fusion), kind=kLoop, calls=%fused_computation | loop fusion | flops 42467328 | bytes 70817280 | tf_op jit(solution)/shard_map/while/body/eval_jaxpr/convert_element_type | solution.py:85
  250.4 9.4 %multiply_convert_fusion.1 = bf16[12,64,1536]{2,1,0:T(8,128)(2,1)} fusion(bf16[384,12,64]{0,2,1:T(8,128)(2,1)} %bitcast.132, bf16[12,384,1536]{2,1,0:T(8,128)(2,1)} %multiply_convert_fusion), kind=kOutput, calls=%fused_computation.10 | convolution fusion | flops 908328960 | bytes 17104896 | tf_op jit(solution)/shard_map/while/body/eval_jaxpr/hqk,qhd->khd/dot_general | solution.py:90
  259.8 12.1 %copy.50 = bf16[1,1536,768]{2,0,1:T(2,128)(2,1)} copy(bf16[1,1536,768]{1,2,0:T(8,128)(2,1)} %bitcast.130) | data formatting | bytes 4718592
  271.9 4.2 copy.65
  276.3 8.1 %fusion.40 = f32[3072,768]{1,0:T(8,128)} fusion(bf16[384,3072]{1,0:T(8,128)(2,1)} %get-tuple-element.132, bf16[1,384,768]{2,1,0:T(8,128)(2,1)} %param.17), kind=kOutput, calls=%fused_computation.86 | convolution fusion | flops 1811939328 | bytes 12386304 | tf_op jit(solution)/shard_map/dot_general | solution.py:35
  285.1 8.5 %fusion.63 = f32[768,3072]{1,0:T(8,128)} fusion(bf16[384,3072]{1,0:T(8,128)(2,1)} %copy-done.12, f32[384,768]{1,0:T(8,128)} %copy-done.5, f32[768]{0:T(1024)S(1)} %copy-done.16, f32[768]{0:T(1024)S(1)} %copy-done.15, f32[384]{0:T(512)S(1)} %copy-done.22, f32[384]{0:T(512)S(1)} %broadcast_multiply_fusion.4), kind=kOutput, calls=%fused_computation.115 | convolution fusion | flops 1813413888 | bytes 12985344 | tf_op jit(solution)/shard_map/dot_general | solution.py:35
  293.7 11.0 %fusion.18 = bf16[12,64,384]{2,1,0:T(8,128)(2,1)} fusion(bf16[1536,12,64]{0,2,1:T(8,128)(2,1)} %bitcast.125, bf16[12,384,1536]{2,1,0:T(8,128)(2,1)} %multiply_convert_fusion), kind=kOutput, calls=%fused_computation.50 | convolution fusion | flops 906559488 | bytes 17104896 | tf_op jit(solution)/shard_map/while/body/eval_jaxpr/hqk,khd->qhd/dot_general | solution.py:87
  310.9 4.5 copy.53
  315.4 7.6 %reduce-scatter.31.cloned.1.call-done = bf16[384,768]{1,0:T(8,128)(2,1)} async-done(((bf16[1536,768]{1,0:T(8,128)(2,1)}), bf16[384,768]{1,0:T(8,128)(2,1)}) %reduce-scatter.31.cloned.1.call-update) | async-done | bytes 589840
  325.6 4.5 copy.51
  330.2 8.1 %fusion.36 = f32[768,2304]{1,0:T(8,128)} fusion(bf16[1,384,768]{2,1,0:T(8,128)(2,1)} %param.16, f32[768]{0:T(1024)S(1)} %copy-done.18, f32[768]{0:T(1024)S(1)} %copy-done.17, f32[384]{0:T(512)S(1)} %copy-done.24, f32[384]{0:T(512)S(1)} %copy-done.20, bf16[1,384,768]{1,2,0:T(8,128)(2,1)} %copy.53, bf16[1,384,768]{1,2,0:T(8,128)(2,1)} %copy.51, ...), kind=kOutput, calls=%fused_computation.84 | convolution fusion | flops 1366032384 | bytes 9446400 | tf_op jit(solution)/shard_map/dot_general | solution.py:35
  338.4 64.4 %reduce-scatter.29.cloned.1.call-done = f32[384,768]{1,0:T(8,128)} async-done(((f32[3072,768]{1,0:T(8,128)}), f32[384,768]{1,0:T(8,128)}) %reduce-scatter.29.cloned.1.call-update) | async-done | bytes 1179664 | tf_op jit(solution)/shard_map/reduce_scatter | solution.py:233
  407.1 76.1 %reduce-scatter.25.cloned.1.call-done = f32[96,3072]{1,0:T(8,128)} async-done(((f32[768,3072]{1,0:T(8,128)}), f32[96,3072]{1,0:T(8,128)}) %reduce-scatter.25.cloned.1.call-update) | async-done | bytes 1179664 | tf_op jit(solution)/shard_map/reduce_scatter | solution.py:232
  485.7 6.2 fusion.19
  491.8 13.6 %reduce-scatter.37.cloned.1.call-done = bf16[192,96]{1,0:T(8,128)(2,1)} async-done(((bf16[768,96]{1,0:T(8,128)(2,1)}), bf16[192,96]{1,0:T(8,128)(2,1)}) %reduce-scatter.37.cloned.1.call-update) | async-done | bytes 36880
  511.4 3.5 fusion.27
  514.9 57.9 %reduce-scatter.21.cloned.1.call-done = f32[96,2304]{1,0:T(8,128)} async-done(((f32[768,2304]{1,0:T(8,128)}), f32[96,2304]{1,0:T(8,128)}) %reduce-scatter.21.cloned.1.call-update) | async-done | bytes 884752 | tf_op jit(solution)/shard_map/reduce_scatter | solution.py:230
  579.0 41.6 %all-reduce = (f32[768]{0:T(1024)}, f32[768]{0:T(1024)}, f32[768]{0:T(1024)}, f32[3072]{0:T(1024)}, f32[768]{0:T(1024)}, /*index=5*/f32[768]{0:T(1024)}, f32[768]{0:T(1024)}, f32[768]{0:T(1024)}, f32[768]{0:T(1024)}) all-reduce(f32[768]{0:T(1024)} %get-tuple-element.116, ...), channel_id=1, replica_groups=mesh['cube'=8,'spec'=4] {'cube','spec'}, use_global_device_ids=true, to_apply=%region_16.17 | all-reduce | flops 9216 | bytes 73728 | tf_op jit(solution)/shard_map/psum | solution.py:214
  630.3 12.2 %reduce-scatter.35.cloned.1.call-done = bf16[576,96]{1,0:T(8,128)(2,1)} async-done(((bf16[2304,96]{1,0:T(8,128)(2,1)}), bf16[576,96]{1,0:T(8,128)(2,1)}) %reduce-scatter.35.cloned.1.call-update) | async-done | bytes 110608
  (141 shorter events, 66.8 us)
Async XLA Ops:
  7.2 61.6 %all-gather.7.cloned.1.call-start = ((), (), s32[]{:S(2)}) async-start(), calls=%async_computation.16 | async-start | bytes 2949120 | tf_op jit(solution)/shard_map/all_gather | solution.py:150
  10.0 5.5 copy-start.26
  10.0 5.5 copy-start.27
  15.5 104.8 %all-gather.5.cloned.1.call-start = ((), (), s32[]{:S(2)}) async-start(), calls=%async_computation.15 | async-start | bytes 2949120 | tf_op jit(solution)/shard_map/all_gather | solution.py:151
  18.4 286.3 %reduce-scatter.23.cloned.1.call-start = ((), (), s32[]{:S(2)}) async-start(), calls=%async_computation.11 | async-start | bytes 2654208 | tf_op jit(solution)/shard_map/reduce_scatter | solution.py:231
  124.6 13.0 %copy-start.3 = (bf16[1,384,768]{2,1,0:T(8,128)(2,1)S(1)}, bf16[1,384,768]{2,1,0:T(8,128)(2,1)}, u32[]{:S(2)}) copy-start(bf16[1,384,768]{2,1,0:T(8,128)(2,1)} %param.16) | copy-start | bytes 1769476
  124.6 13.0 %copy-start.13 = (bf16[768,768]{1,0:T(8,128)(2,1)S(1)}, bf16[768,768]{1,0:T(8,128)(2,1)}, u32[]{:S(2)}) copy-start(bf16[768,768]{1,0:T(8,128)(2,1)} %param.22) | copy-start | bytes 3538948
  124.6 13.0 %copy-start.29 = (f32[768]{0:T(1024)S(1)}, f32[768]{0:T(1024)}, u32[]{:S(2)}) copy-start(f32[768]{0:T(1024)} %param.23) | copy-start | bytes 9220
  137.6 17.5 %slice-start.2 = ((s8[4718592]{0:T(1024)(128)(4,1)}), s8[4194304]{0:T(1024)(128)(4,1)S(1)}, s32[]{:S(2)}) async-start(s8[4718592]{0:T(1024)(128)(4,1)} %bitcast.151), calls=%async_computation.24 | async-start | bytes 8388608
  137.6 23.4 %slice-start = ((s8[4718592]{0:T(1024)(128)(4,1)}), s8[4194304]{0:T(1024)(128)(4,1)S(1)}, s32[]{:S(2)}) async-start(s8[4718592]{0:T(1024)(128)(4,1)} %bitcast.149), calls=%async_computation.22 | async-start | bytes 8388608
  138.4 25.4 %copy-start.5 = (f32[384,768]{1,0:T(8,128)}, f32[384,768]{1,0:T(8,128)S(1)}, u32[]{:S(2)}) copy-start(f32[384,768]{1,0:T(8,128)S(1)} %get-tuple-element.140) | copy-start | bytes 3538948
  138.7 25.1 %copy-start.21 = (f32[384]{0:T(512)}, f32[384]{0:T(512)S(1)}, u32[]{:S(2)}) copy-start(f32[384]{0:T(512)S(1)} %add_rsqrt_fusion) | copy-start | bytes 4612
  138.7 16.4 %copy-start.11 = (bf16[1,384,768]{2,1,0:T(8,128)(2,1)S(1)}, bf16[1,384,768]{2,1,0:T(8,128)(2,1)}, u32[]{:S(2)}) copy-start(bf16[1,384,768]{2,1,0:T(8,128)(2,1)} %param.17) | copy-start | bytes 1769476
  138.7 16.4 %slice-start.3 = ((s8[4718592]{0:T(1024)(128)(4,1)}), s8[524288]{0:T(1024)(128)(4,1)S(1)}, s32[]{:S(2)}) async-start(s8[4718592]{0:T(1024)(128)(4,1)} %bitcast.151), calls=%async_computation.25 | async-start | bytes 1048576
  138.7 22.2 %slice-start.1 = ((s8[4718592]{0:T(1024)(128)(4,1)}), s8[524288]{0:T(1024)(128)(4,1)S(1)}, s32[]{:S(2)}) async-start(s8[4718592]{0:T(1024)(128)(4,1)} %bitcast.149), calls=%async_computation.23 | async-start | bytes 1048576
  170.8 137.4 %reduce-scatter.33.cloned.1.call-start = ((), (), s32[]{:S(2)}) async-start(), calls=%async_computation.18 | async-start | bytes 2949120
  226.2 96.8 %reduce-scatter.31.cloned.1.call-start = ((), (), s32[]{:S(2)}) async-start(), calls=%async_computation.17 | async-start | bytes 2949120
  276.1 126.7 %reduce-scatter.29.cloned.1.call-start = ((), (), s32[]{:S(2)}) async-start(), calls=%async_computation.14 | async-start | bytes 10616832 | tf_op jit(solution)/shard_map/reduce_scatter | solution.py:233
  284.4 198.7 %reduce-scatter.25.cloned.1.call-start = ((), (), s32[]{:S(2)}) async-start(), calls=%async_computation.12 | async-start | bytes 10616832 | tf_op jit(solution)/shard_map/reduce_scatter | solution.py:232
  293.6 211.9 %reduce-scatter.37.cloned.1.call-start = ((), (), s32[]{:S(2)}) async-start(), calls=%async_computation.20 | async-start | bytes 245760
  308.1 22.0 %copy-start.17 = (f32[768]{0:T(1024)S(1)}, f32[768]{0:T(1024)}, u32[]{:S(2)}) copy-start(f32[768]{0:T(1024)} %param.28) | copy-start | bytes 9220
  308.1 22.0 %copy-start.18 = (f32[768]{0:T(1024)S(1)}, f32[768]{0:T(1024)}, u32[]{:S(2)}) copy-start(f32[768]{0:T(1024)} %param.29) | copy-start | bytes 9220
  308.1 22.0 %copy-start.20 = (f32[384]{0:T(512)S(1)}, f32[384]{0:T(512)}, u32[]{:S(2)}) copy-start(f32[384]{0:T(512)} %copy-done.19) | copy-start | bytes 4612
  308.1 22.0 %copy-start.24 = (f32[384]{0:T(512)S(1)}, f32[384]{0:T(512)}, u32[]{:S(2)}) copy-start(f32[384]{0:T(512)} %copy-done.23) | copy-start | bytes 4612
  308.1 264.6 %reduce-scatter.21.cloned.1.call-start = ((), (), s32[]{:S(2)}) async-start(), calls=%async_computation.10 | async-start | bytes 7962624 | tf_op jit(solution)/shard_map/reduce_scatter | solution.py:230
  338.3 147.4 %copy-start.30 = (f32[768]{0:T(1024)S(1)}, f32[768]{0:T(1024)}, u32[]{:S(2)}) copy-start(f32[768]{0:T(1024)} %param.27) | copy-start | bytes 9220
  338.3 286.9 %reduce-scatter.39.cloned.1.call-start = ((), (), s32[]{:S(2)}) async-start(), calls=%async_computation.21 | async-start | bytes 737280
  407.1 221.6 %reduce-scatter.27.cloned.1.call-start = ((), (), s32[]{:S(2)}) async-start(), calls=%async_computation.13 | async-start | bytes 737280 | tf_op jit(solution)/shard_map/reduce_scatter | solution.py:242
  485.4 157.1 %reduce-scatter.35.cloned.1.call-start = ((), (), s32[]{:S(2)}) async-start(), calls=%async_computation.19 | async-start | bytes 737280
  507.0 4.4 copy-start.7
  507.0 4.4 copy-start.8
  514.9 64.1 %copy-start.25 = (f32[768]{0:T(1024)S(1)}, f32[768]{0:T(1024)}, u32[]{:S(2)}) copy-start(f32[768]{0:T(1024)} %get-tuple-element.130) | copy-start | bytes 9220
  (15 other events, 42.2 us)
Sparse Core Ops, SparseCore 0:
  15.6 53.1 all-gather.6
  71.0 49.2 all-gather.4
  171.0 41.3 reduce-scatter.22
  226.3 46.4 reduce-scatter.32
  276.2 46.7 reduce-scatter.30
  326.7 75.9 reduce-scatter.28
  406.6 76.4 reduce-scatter.24
  486.1 19.3 reduce-scatter.36
  509.0 63.7 reduce-scatter.20
  575.0 22.0 reduce-scatter.38
  599.5 20.3 reduce-scatter.26
  622.1 20.3 reduce-scatter.34
where the time goes:
time: 663 us; the launch traced here: 653 us
  waiting for transfers between devices  298 us (45%)
  matrix products  154 us (23%)
  local copies, waits for them, and re-layouts  76 us (11%)
  other arithmetic  67.3 us (10%)
  blocking collectives  41.6 us (6%)
  between operations  15.7 us (2%)
    reduce_scatter x1, waiting for transfers between devices, local(): lax.psum_scatter(matrices[2], 'cube', scatter_dimension=0, tiled=True)  76.1 us
    reduce_scatter x1, waiting for transfers between devices, local(): lax.psum_scatter(matrices[3], 'cube', scatter_dimension=0, tiled=True)  64.4 us
    unnamed x85, local copies, waits for them, and re-layouts  62.3 us
    reduce_scatter x1, waiting for transfers between devices, local(): lax.psum_scatter(matrices[0], 'cube', scatter_dimension=0, tiled=True)  57.9 us
    all_gather x1, waiting for transfers between devices, local(): lax.all_gather(key_part, 'spec', axis=1, tiled=True)  47.6 us
    psum x1, blocking collectives, local(): lax.psum((grad_query_bias, grad_value_bias, grad_output_bias, grad_up_bia...  41.6 us
    unnamed x17, waiting for transfers between devices  33.6 us
    dot_general x4, matrix products, left_dot(): lax.dot_general(left, right, (((0,), (0,)), ((), ())), preferred_element_...  26.9 us
  transfers between devices with their start and end apart: 12, of which 8 were waited for; matrix products, arithmetic and copies ran while one was open for 36% of the time, Pallas kernels for 0%

commit v1 on v0

v1 whole, which is shorter than its diff:
```python
import math
from functools import partial

import jax
import jax.numpy as jnp
import numpy as np
from jax import lax
from jax.experimental import pallas as pl
from jax.experimental.pallas import tpu as pltpu
from jax.sharding import PartitionSpec as P

HEADS = 12
HD = 64
PAIRS = HEADS // 2
EPS = 1e-06
SCALE = HD ** (-0.5)
TO_EXP2 = SCALE * math.log2(math.e)
MASKED = -1e30

BF = jnp.bfloat16
F32 = jnp.float32


def dot(left, right):
    return jnp.dot(left, right, preferred_element_type=F32)


def dot_nt(left, right):
    return lax.dot_general(left, right, (((1,), (1,)), ((), ())), preferred_element_type=F32)


def dot_tn(left, right):
    return lax.dot_general(left, right, (((0,), (0,)), ((), ())), preferred_element_type=F32)


def normalize(values):
    average = jnp.mean(values, -1, keepdims=True)
    centred = values - average
    inverse = lax.rsqrt(jnp.mean(centred * centred, -1, keepdims=True) + EPS)
    return centred * inverse, inverse


def transposed(values):
    return values.astype(F32).T


def params(megabytes):
    return pltpu.CompilerParams(vmem_limit_bytes=megabytes * 2**20)


def cost(flops, nbytes, trans=0):
    return pl.CostEstimate(flops=flops, bytes_accessed=nbytes, transcendentals=trans)


def extra_lanes(where_ref, rows, ones):
    slot = lax.broadcasted_iota(jnp.int32, (rows, 128), 0) + where_ref[0]
    lane = lax.broadcasted_iota(jnp.int32, (rows, 128), 1)
    masked = jnp.where(slot < where_ref[1], 0.0, MASKED)
    rest = jnp.where(lane <= ones, 1.0, 0.0)
    return jnp.where(lane == 0, masked, rest).astype(BF)


def two_heads(part, extra):
    n = part.shape[1]
    zero = jnp.zeros((HD, n), part.dtype)
    left = jnp.concatenate([part[:HD], zero], 0)
    right = jnp.concatenate([zero, part[HD:]], 0)
    return jnp.concatenate([jnp.concatenate([left, right], 1), extra], 0)


def pair_lanes(pair):
    return slice(pair * 2 * HD, (pair + 1) * 2 * HD)


def forward_kernel(first, last, *refs):
    if first:
        where_ref, tok_ref, gain_ref, shift_ref, w_ref, qb_ref, vb_ref = refs[:7]
        outs = refs[7:]
        h_out, k_out, v_out, m_out, l_out, acc_out, q_out, qt_out = outs
    else:
        where_ref, tok_ref, gain_ref, shift_ref, w_ref, vb_ref, qt_ref, m_ref, l_ref, acc_ref = refs[:10]
        h_out, k_out, v_out, m_out, l_out, acc_out = refs[10:]
    rows, width = tok_ref.shape
    normed, _ = normalize(tok_ref[...].astype(F32))
    hidden = (normed * gain_ref[...] + shift_ref[...]).astype(BF)
    h_out[...] = hidden
    k_out[...] = dot(hidden, w_ref[:, width : 2 * width]).astype(BF)
    values = dot(hidden, w_ref[:, 2 * width :]) + vb_ref[...]
    v_out[...] = values.astype(BF)
    values_t = v_out[...].astype(F32).T.astype(BF)
    if first:
        q_out[...] = (dot(hidden, w_ref[:, :width]) + qb_ref[...]).astype(BF)
        qt_out[...] = q_out[...].astype(F32).T.astype(BF)
        qt_ref = qt_out
    extra_keys = extra_lanes(where_ref, rows, 0)
    ones_row = (lax.broadcasted_iota(jnp.int32, (128, 2 * rows), 0) == 0).astype(BF)
    for pair in range(PAIRS):
        lanes = pair_lanes(pair)
        keys = jnp.concatenate([k_out[:, lanes], extra_keys], 1)
        scores = dot(keys, two_heads(qt_ref[lanes, :], ones_row))
        top = jnp.max(scores, 0, keepdims=True)
        if not first:
            before = m_ref[pair : pair + 1, :]
            top = jnp.maximum(top, before)
            fade = jnp.exp2((before - top) * TO_EXP2)
        weights = jnp.exp2((scores - top) * TO_EXP2)
        total = jnp.sum(weights, 0, keepdims=True)
        if not first:
            total = total + l_ref[pair : pair + 1, :] * fade
        both = dot(values_t[lanes, :], weights.astype(BF))
        for head in range(2):
            own = slice(lanes.start + head * HD, lanes.start + (head + 1) * HD)
            cols = slice(head * rows, (head + 1) * rows)
            part = both[head * HD : (head + 1) * HD, cols]
            if not first:
                part = part + acc_ref[own, :] * fade[:, cols]
            if last:
                part = part / total[:, cols]
            acc_out[own, :] = part
        if last:
            m_out[pair : pair + 1, :] = -(top + jnp.log2(total) * (1.0 / TO_EXP2))
        else:
            m_out[pair : pair + 1, :] = top
        l_out[pair : pair + 1, :] = total


def forward_step(first, last, where, tok, gain, shift, w, qb, vb, state):
    rows, width = tok.shape
    block = jax.ShapeDtypeStruct((rows, width), BF)
    outs = [
        block,
        block,
        block,
        jax.ShapeDtypeStruct((8, 2 * rows), F32),
        jax.ShapeDtypeStruct((8, 2 * rows), F32),
        jax.ShapeDtypeStruct((width, rows), F32),
    ]
    vmem = pl.BlockSpec(memory_space=pltpu.VMEM)
    smem = pl.BlockSpec(memory_space=pltpu.SMEM)
    if first:
        outs += [block, jax.ShapeDtypeStruct((width, rows), BF)]
        args = (where, tok, gain, shift, w, qb, vb)
    else:
        args = (where, tok, gain, shift, w, vb) + tuple(state)
    flops = 2 * rows * width * width * (3 if first else 2) + 4 * rows * rows * width * 4
    return pl.pallas_call(
        partial(forward_kernel, first, last),
        out_shape=outs,
        in_specs=[smem] + [vmem] * (len(args) - 1),
        out_specs=[vmem] * len(outs),
        compiler_params=params(32),
        cost_estimate=cost(flops, 12 * 2**20, HEADS * rows * rows),
        name="attend_first" if first else ("attend_last" if last else "attend_next"),
    )(*args)


def middle_kernel(
    order_ref,
    tok_ref,
    cot_ref,
    attt_ref,
    wo_ref,
    ob_ref,
    gain_ref,
    shift_ref,
    up_ref,
    ub_ref,
    down_ref,
    db_ref,
    perm_ref,
    block_out,
    down_keep,
    down_send,
    up_keep,
    up_send,
    out_keep,
    out_send,
    da_out,
    dat_out,
    negd_out,
    gmid_out,
    vec_out,
    ubg_out,
    mid_ref,
    norm_ref,
    inv_ref,
    h2_ref,
    h2t_ref,
    att_ref,
    res_ref,
    gh_ref,
):
    step = pl.program_id(0)
    steps = pl.num_programs(0)
    rows, width = tok_ref.shape

    @pl.when(step == 0)
    def _():
        att_ref[...] = attt_ref[...].T.astype(BF)
        middle = tok_ref[...].astype(F32) + (dot(att_ref[...], wo_ref[...]) + ob_ref[...])
        mid_ref[...] = middle
        normed, inverse = normalize(middle)
        norm_ref[...] = normed
        inv_ref[...] = jnp.broadcast_to(inverse, inv_ref.shape)
        h2_ref[...] = (normed * gain_ref[...] + shift_ref[...]).astype(BF)
        h2t_ref[...] = dot_nt(perm_ref[...], h2_ref[...]).astype(BF)
        res_ref[...] = jnp.zeros_like(res_ref)
        gh_ref[...] = jnp.zeros_like(gh_ref)

    before = dot(h2_ref[...], up_ref[...]) + ub_ref[...]
    cdf = 0.5 * (1.0 + lax.erf(before * math.sqrt(0.5)))
    slope = cdf + before * (jnp.exp(-0.5 * before * before) * (1.0 / math.sqrt(2.0 * math.pi)))
    lifted = (before * cdf).astype(BF)
    res_ref[...] += dot(lifted, down_ref[...])
    grad_down = dot_tn(lifted, cot_ref[...]).astype(BF)

    @pl.when(step < steps // 2)
    def _():
        down_send[...] = grad_down

    @pl.when(step >= steps // 2)
    def _():
        down_keep[...] = grad_down

    grad_lifted = dot_nt(cot_ref[...], down_ref[...])
    grad_before = (grad_lifted * slope).astype(BF)
    ubg_out[...] = jnp.sum(grad_before.astype(F32), 0, keepdims=True)
    grad_up = dot(h2t_ref[...], grad_before).astype(BF)
    half = width // 2
    up_keep[...] = grad_up[:half]
    up_send[...] = grad_up[half:]
    gh_ref[...] += dot_nt(grad_before, up_ref[...])

    @pl.when(step == steps - 1)
    def _():
        block_out[...] = (mid_ref[...] + (res_ref[...] + db_ref[...])).astype(BF)
        cot = cot_ref[...].astype(F32)
        grad = gh_ref[...]
        normed = norm_ref[...]
        vec_out[0:1, :] = jnp.sum(cot, 0, keepdims=True)
        vec_out[1:2, :] = jnp.sum(grad * normed, 0, keepdims=True)
        vec_out[2:3, :] = jnp.sum(grad, 0, keepdims=True)
        scaled = grad * gain_ref[...]
        grad_middle = cot + inv_ref[:, :1] * (
            scaled
            - jnp.mean(scaled, -1, keepdims=True)
            - normed * jnp.mean(scaled * normed, -1, keepdims=True)
        )
        gmid_out[...] = grad_middle
        branch = grad_middle.astype(BF)
        vec_out[3:4, :] = jnp.sum(branch.astype(F32), 0, keepdims=True)
        att_t = dot_nt(perm_ref[...], att_ref[...]).astype(BF)
        grad_out = dot(att_t, branch).astype(BF)
        out_keep[...] = grad_out[:half]
        out_send[...] = grad_out[half:]
        grad_att = dot_nt(branch, wo_ref[...]).astype(BF)
        da_out[...] = grad_att
        grad_att_t = grad_att.astype(F32).T
        dat_out[...] = grad_att_t.astype(BF)
        product = grad_att_t * attt_ref[...]
        for head in range(HEADS):
            spread = jnp.sum(product[head * HD : (head + 1) * HD], 0, keepdims=True)
            place = slice((head % 2) * rows, (head % 2 + 1) * rows)
            negd_out[head // 2 : head // 2 + 1, place] = -spread


def middle_step(order, tok, cot, attt, wo, ob, gain, shift, up, ub, down, db, perm):
    rows, width = tok.shape
    hidden = up.shape[1]
    steps = 8
    chunk = hidden // steps
    half = steps // 2

    def whole(shape):
        return pl.BlockSpec(shape, lambda i, order: (0,) * len(shape))

    in_specs = [
        whole((rows, width)),
        whole((rows, width)),
        whole((width, rows)),
        whole((width, width)),
        whole((1, width)),
        whole((1, width)),
        whole((1, width)),
        pl.BlockSpec((width, chunk), lambda i, order: (0, order[i])),
        pl.BlockSpec((1, chunk), lambda i, order: (0, order[i])),
        pl.BlockSpec((chunk, width), lambda i, order: (order[i], 0)),
        whole((1, width)),
        whole((width, width)),
    ]
    out_shape = [
        jax.ShapeDtypeStruct((rows, width), BF),
        jax.ShapeDtypeStruct((hidden // 2, width), BF),
        jax.ShapeDtypeStruct((hidden // 2, width), BF),
        jax.ShapeDtypeStruct((width // 2, hidden), BF),
        jax.ShapeDtypeStruct((width // 2, hidden), BF),
        jax.ShapeDtypeStruct((width // 2, width), BF),
        jax.ShapeDtypeStruct((width // 2, width), BF),
        jax.ShapeDtypeStruct((rows, width), BF),
        jax.ShapeDtypeStruct((width, rows), BF),
        jax.ShapeDtypeStruct((8, 2 * rows), F32),
        jax.ShapeDtypeStruct((rows, width), F32),
        jax.ShapeDtypeStruct((8, width), F32),
        jax.ShapeDtypeStruct((1, hidden), F32),
    ]
    out_specs = [
        whole((rows, width)),
        pl.BlockSpec((chunk, width), lambda i, order: (jnp.maximum(i - half, 0), 0)),
        pl.BlockSpec((chunk, width), lambda i, order: (jnp.minimum(i, half - 1), 0)),
        pl.BlockSpec((width // 2, chunk), lambda i, order: (0, order[i])),
        pl.BlockSpec((width // 2, chunk), lambda i, order: (0, order[i])),
        whole((width // 2, width)),
        whole((width // 2, width)),
        whole((rows, width)),
        whole((width, rows)),
        whole((8, 2 * rows)),
        whole((rows, width)),
        whole((8, width)),
        pl.BlockSpec((1, chunk), lambda i, order: (0, order[i])),
    ]
    return pl.pallas_call(
        middle_kernel,
        out_shape=out_shape,
        grid_spec=pltpu.PrefetchScalarGridSpec(
            num_scalar_prefetch=1,
            grid=(steps,),
            in_specs=in_specs,
            out_specs=out_specs,
            scratch_shapes=[
                pltpu.VMEM((rows, width), F32),
                pltpu.VMEM((rows, width), F32),
                pltpu.VMEM((rows, 128), F32),
                pltpu.VMEM((rows, width), BF),
                pltpu.VMEM((width, rows), BF),
                pltpu.VMEM((rows, width), BF),
                pltpu.VMEM((rows, width), F32),
                pltpu.VMEM((rows, width), F32),
            ],
        ),
        compiler_params=params(48),
        cost_estimate=cost(12 * rows * width * hidden + 6 * rows * width * width, 30 * 2**20, 0),
        name="middle",
    )(order, tok, cot, attt, wo, ob, gain, shift, up, ub, down, db, perm)


def three_parts(row):
    high = row.astype(BF)
    rest = row - high.astype(F32)
    mid = rest.astype(BF)
    low = (rest - mid.astype(F32)).astype(BF)
    return high.astype(F32), mid.astype(F32), low.astype(F32)


def extra_rows(row, with_mask):
    n = row.shape[1]
    high, mid, low = three_parts(row)
    place = lax.broadcasted_iota(jnp.int32, (128, n), 0)
    out = jnp.where(place == 0, 1.0 if with_mask else 0.0, 0.0)
    out = jnp.where(place == 1, high, out)
    out = jnp.where(place == 2, mid, out)
    out = jnp.where(place == 3, low, out)
    return out.astype(BF)


def backward_kernel(first, last, *refs):
    (where_ref, q_ref, qt_ref, da_ref, dat_ref, negl_ref, negd_ref, k_ref, v_ref, tok_ref, w_ref) = refs[:11]
    refs = refs[11:]
    if not first:
        dqt_ref, vec_ref = refs[:2]
        refs = refs[2:]
    if last:
        dkv_out, g_out, vec_out, dq_out = refs[:4]
        (dqt_out,) = refs[4:]
    else:
        dkv_out, g_out, vec_out, dqt_out = refs
    rows, width = q_ref.shape
    extra_keys = extra_lanes(where_ref, rows, 3)
    keys_t = k_ref[...].astype(F32).T.astype(BF)
    lane = lax.broadcasted_iota(jnp.int32, (rows, 128), 1)
    for pair in range(PAIRS):
        lanes = pair_lanes(pair)
        keys = jnp.concatenate([k_ref[:, lanes], extra_keys], 1)
        scores = dot(keys, two_heads(qt_ref[lanes, :], extra_rows(negl_ref[pair : pair + 1, :], True)))
        softmaxed = jnp.exp2(scores * TO_EXP2)
        values = jnp.concatenate([v_ref[:, lanes], extra_keys], 1)
        centred = dot(values, two_heads(dat_ref[lanes, :], extra_rows(negd_ref[pair : pair + 1, :], False)))
        grad_scores = (softmaxed * centred).astype(BF)
        weights = softmaxed.astype(BF)
        zero = jnp.zeros((rows, 128), BF)
        q_pair = q_ref[:, lanes]
        da_pair = da_ref[:, lanes]
        q_both = jnp.concatenate([jnp.where(lane < HD, q_pair, zero), jnp.where(lane < HD, zero, q_pair)], 0)
        da_both = jnp.concatenate([jnp.where(lane < HD, da_pair, zero), jnp.where(lane < HD, zero, da_pair)], 0)
        dkv_out[:, lanes] = (dot(grad_scores, q_both) * SCALE).astype(BF)
        dkv_out[:, slice(width + lanes.start, width + lanes.stop)] = dot(weights, da_both).astype(BF)
        both = dot(keys_t[lanes, :], grad_scores)
        for head in range(2):
            own = slice(lanes.start + head * HD, lanes.start + (head + 1) * HD)
            part = both[head * HD : (head + 1) * HD, head * rows : (head + 1) * rows]
            if not first:
                part = part + dqt_ref[own, :]
            dqt_out[own, :] = part
    grad = dot_nt(dkv_out[...], w_ref[:, width:])
    query_bias = jnp.zeros((1, width), F32)
    if last:
        dq = (dqt_out[...].T * SCALE).astype(BF)
        dq_out[...] = dq
        query_bias = jnp.sum(dq.astype(F32), 0, keepdims=True)
        grad = grad + dot_nt(dq, w_ref[:, :width])
    g_out[...] = grad.astype(g_out.dtype)
    normed, _ = normalize(tok_ref[...].astype(F32))
    value_bias = jnp.sum(dkv_out[:, width:].astype(F32), 0, keepdims=True)
    gain = jnp.sum(grad * normed, 0, keepdims=True)
    shift = jnp.sum(grad, 0, keepdims=True)
    if not first:
        value_bias = value_bias + vec_ref[1:2, :]
        gain = gain + vec_ref[2:3, :]
        shift = shift + vec_ref[3:4, :]
    vec_out[0:1, :] = query_bias
    vec_out[1:2, :] = value_bias
    vec_out[2:3, :] = gain
    vec_out[3:4, :] = shift
    vec_out[4:8, :] = jnp.zeros((4, width), F32)


def backward_step(first, last, where, q, qt, da, dat, negl, negd, k, v, tok, w, state):
    rows, width = q.shape
    vmem = pl.BlockSpec(memory_space=pltpu.VMEM)
    smem = pl.BlockSpec(memory_space=pltpu.SMEM)
    args = (where, q, qt, da, dat, negl, negd, k, v, tok, w) + (() if first else tuple(state))
    outs = [
        jax.ShapeDtypeStruct((rows, 2 * width), BF),
        jax.ShapeDtypeStruct((rows, width), F32 if last else BF),
        jax.ShapeDtypeStruct((8, width), F32),
    ]
    if last:
        outs.append(jax.ShapeDtypeStruct((rows, width), BF))
        scratch = [pltpu.VMEM((width, rows), F32)]
    else:
        outs.append(jax.ShapeDtypeStruct((width, rows), F32))
        scratch = []
    flops = 2 * rows * width * width * (3 if last else 2) + 10 * rows * rows * width * 4
    return pl.pallas_call(
        partial(backward_kernel, first, last),
        out_shape=outs,
        in_specs=[smem] + [vmem] * (len(args) - 1),
        out_specs=[vmem] * len(outs),
        scratch_shapes=scratch,
        compiler_params=params(40),
        cost_estimate=cost(flops, 16 * 2**20, HEADS * rows * rows),
        name="attend_back",
    )(*args)


def projection_kernel(*refs):
    count = (len(refs) - 5) // 2
    perm_ref, dq_ref = refs[:2]
    hiddens = refs[2 : 2 + count]
    dkvs = refs[2 + count : 2 + 2 * count]
    keep_ref, send_ref, ht_ref = refs[2 + 2 * count :]
    step = pl.program_id(0)
    rows = hiddens[0].shape[0]
    half = keep_ref.shape[0]

    @pl.when(step == 0)
    def _():
        for i, hidden in enumerate(hiddens):
            ht_ref[:, i * rows : (i + 1) * rows] = dot_nt(perm_ref[...], hidden[...]).astype(BF)

    @pl.when(step < 2)
    def _():
        grad = dot(ht_ref[:, :rows], dq_ref[...])
        keep_ref[...] = grad[:half].astype(BF)
        send_ref[...] = grad[half:].astype(BF)

    @pl.when(step >= 2)
    def _():
        right = jnp.concatenate([dkv[...] for dkv in dkvs], 0)
        grad = dot(ht_ref[...], right)
        keep_ref[...] = grad[:half].astype(BF)
        send_ref[...] = grad[half:].astype(BF)


def projection_step(perm, dq, hiddens, dkvs):
    rows, width = dq.shape
    chunk = width // 2
    count = len(hiddens)

    def whole(shape):
        return pl.BlockSpec(shape, lambda i: (0,) * len(shape))

    out = jax.ShapeDtypeStruct((width // 2, 3 * width), BF)
    return pl.pallas_call(
        projection_kernel,
        out_shape=[out, out],
        grid=(6,),
        in_specs=[whole((width, width)), pl.BlockSpec((rows, chunk), lambda i: (0, jnp.minimum(i, 1)))]
        + [whole((rows, width))] * count
        + [pl.BlockSpec((rows, chunk), lambda i: (0, jnp.maximum(i - 2, 0)))] * count,
        out_specs=[pl.BlockSpec((width // 2, chunk), lambda i: (0, i))] * 2,
        scratch_shapes=[pltpu.VMEM((width, count * rows), BF)],
        compiler_params=params(32),
        cost_estimate=cost(2 * rows * width * width * (1 + 2 * count), 12 * 2**20, 0),
        name="projection_grad",
    )(perm, dq, *hiddens, *dkvs)


def final_kernel(tok_ref, gain_ref, g_ref, recv_ref, gmid_ref, out_ref):
    normed, inverse = normalize(tok_ref[...].astype(F32))
    scaled = (g_ref[...] + recv_ref[...].astype(F32)) * gain_ref[...]
    out_ref[...] = gmid_ref[...] + inverse * (
        scaled
        - jnp.mean(scaled, -1, keepdims=True)
        - normed * jnp.mean(scaled * normed, -1, keepdims=True)
    )


def final_step(tok, gain, g, recv, gmid):
    vmem = pl.BlockSpec(memory_space=pltpu.VMEM)
    return pl.pallas_call(
        final_kernel,
        out_shape=jax.ShapeDtypeStruct(tok.shape, F32),
        in_specs=[vmem] * 5,
        out_specs=vmem,
        compiler_params=params(16),
        cost_estimate=cost(20 * tok.size, 10 * tok.size, 0),
        name="norm_back",
    )(tok, gain, g, recv, gmid)


def flip(count, distance):
    return [(i, i ^ distance) for i in range(count)]


def tree_place(bits):
    n = len(bits)
    return np.array([sum(((p >> (n - 1 - i)) & 1) << bit for i, bit in enumerate(bits)) for p in range(1 << n)])


def tree_sum(keep, recv, bits, cubes):
    for bit in bits:
        half = keep.shape[0] // 2
        send = (keep[half:].astype(F32) + recv[half:].astype(F32)).astype(BF)
        moved = lax.ppermute(send, "cube", flip(cubes, 1 << bit))
        keep = (keep[:half].astype(F32) + recv[:half].astype(F32)).astype(BF)
        recv = moved
    return keep.astype(F32) + recv.astype(F32)


def spec_sum(part, me, count):
    cols = part.shape[1] // count

    def mine(distance):
        return lax.dynamic_slice_in_dim(part, (me ^ distance) * cols, cols, 1)

    got = [lax.ppermute(mine(d).astype(BF), "spec", flip(count, d)) for d in range(1, count)]
    total = mine(0)
    for piece in got:
        total = total + piece.astype(F32)
    return total


def vector_sum(vectors, cubes, count):
    done = 1
    while done < cubes:
        group = min(8, cubes // done)
        got = [lax.ppermute(vectors, "cube", flip(cubes, d * done)) for d in range(1, group)]
        vectors = sum(got, vectors)
        done *= group
    got = [lax.ppermute(vectors, "spec", flip(count, d)) for d in range(1, count)]
    return sum(got, vectors)


def local(
    tokens,
    cotangent,
    lengths,
    projection,
    query_bias,
    value_bias,
    output_weight,
    output_bias,
    up_weight,
    up_bias,
    down_weight,
    down_bias,
    first_gain,
    first_shift,
    second_gain,
    second_shift,
):
    _, rows, width = tokens.shape
    hidden = up_weight.shape[1]
    cubes, count = lax.axis_size("cube"), lax.axis_size("spec")
    cube, spec = lax.axis_index("cube"), lax.axis_index("spec")
    tok = tokens.reshape(rows, width)
    cot = cotangent.reshape(rows, width)

    def row(vector):
        return vector.reshape(1, -1)

    ring = [(i, (i + 1) % count) for i in range(count)]
    blocks = [tok]
    for _ in range(count - 1):
        blocks.append(lax.ppermute(blocks[-1], "spec", ring))
    wheres = [
        jnp.stack([((spec - s) % count).astype(jnp.int32) * rows, lengths[0].astype(jnp.int32)])
        for s in range(count)
    ]

    bits = cubes.bit_length() - 1
    order_a = list(range(bits))
    order_b = [0] + list(range(bits - 1, 0, -1))
    place_a, place_b = tree_place(order_a), tree_place(order_b)
    split = cubes // 2

    def source_rows(place, offset, size, block):
        start = (jnp.asarray(place, jnp.int32) ^ cube) * block + offset
        return (start[:, None] + jnp.arange(size, dtype=jnp.int32)[None, :]).reshape(-1)

    def one_hot(source):
        return (source[:, None] == jnp.arange(width, dtype=jnp.int32)[None, :]).astype(BF)

    block = width // cubes
    part = block // 2
    perm_b = one_hot(source_rows(place_b, 0, block, block))
    perm_mixed = one_hot(
        jnp.concatenate(
            [
                source_rows(place_a[:split], 0, part, block),
                source_rows(place_b[:split], part, part, block),
                source_rows(place_a[split:], 0, part, block),
                source_rows(place_b[split:], part, part, block),
            ]
        )
    )
    chunks = 8
    if cubes == chunks:
        order = jnp.asarray(np.roll(place_a, -split), jnp.int32) ^ cube
    else:
        order = jnp.roll(jnp.arange(chunks, dtype=jnp.int32), -(chunks // 2))

    hiddens, keys, values = [], [], []
    state = None
    for s in range(count):
        first, last = s == 0, s == count - 1
        made = forward_step(
            first,
            last,
            wheres[s],
            blocks[s],
            row(first_gain),
            row(first_shift),
            projection,
            row(query_bias),
            row(value_bias),
            state,
        )
        hiddens.append(made[0])
        keys.append(made[1])
        values.append(made[2])
        if first:
            q, qt = made[6:]
        state = (qt,) + tuple(made[3:6])
    negl, attt = state[1], state[3]

    (
        block_out,
        down_keep,
        down_send,
        up_keep,
        up_send,
        out_keep,
        out_send,
        da,
        dat,
        negd,
        gmid,
        vec_mid,
        grad_up_bias,
    ) = middle_step(
        order,
        tok,
        cot,
        attt,
        output_weight,
        row(output_bias),
        row(second_gain),
        row(second_shift),
        up_weight,
        row(up_bias),
        down_weight,
        row(down_bias),
        perm_b,
    )
    if cubes != chunks:
        whole = jnp.concatenate([down_keep, down_send], 0).reshape(cubes, hidden // cubes, width)
        whole = jnp.take(whole, jnp.asarray(place_a, jnp.int32) ^ cube, axis=0)
        down_keep = whole[:split].reshape(hidden // 2, width)
        down_send = whole[split:].reshape(hidden // 2, width)

    pair = flip(cubes, 1)
    down_recv = lax.ppermute(down_send, "cube", pair)
    up_recv = lax.ppermute(up_send, "cube", pair)
    out_recv = lax.ppermute(out_send, "cube", pair)
    grad_down = tree_sum(down_keep, down_recv, order_a[1:], cubes)
    grad_up = tree_sum(up_keep, up_recv, order_b[1:], cubes)
    grad_out = tree_sum(out_keep, out_recv, order_b[1:], cubes)

    dkvs = [None] * count
    back_state = None
    travelling = None
    for step in range(count):
        s = (step + 1) % count
        first, last = step == 0, step == count - 1
        made = backward_step(
            first,
            last,
            wheres[s],
            q,
            qt,
            da,
            dat,
            negl,
            negd,
            keys[s],
            values[s],
            blocks[s],
            projection,
            back_state,
        )
        dkvs[s] = made[0]
        back_state = (made[3], made[2])
        if last:
            g_own, vec_back, dq = made[1:]
        else:
            g = made[1]
            if not first:
                g = (g.astype(F32) + travelling.astype(F32)).astype(BF)
            travelling = lax.ppermute(g, "spec", ring)

    proj_keep, proj_send = projection_step(perm_mixed, dq, hiddens, dkvs)
    proj_recv = lax.ppermute(proj_send, "cube", pair)
    mid = proj_keep.shape[0] // 2
    proj_a = tree_sum(proj_keep[:mid], proj_recv[:mid], order_a[1:], cubes)
    proj_b = tree_sum(proj_keep[mid:], proj_recv[mid:], order_b[1:], cubes)
    grad_proj = jnp.concatenate([proj_a, proj_b], 0)

    vectors = jnp.concatenate([vec_mid[:4], vec_back[:4], grad_up_bias.reshape(-1, width)], 0)
    vectors = vector_sum(vectors, cubes, count)

    grad_tokens = final_step(tok, row(first_gain), g_own, travelling, gmid)

    return (
        block_out.reshape(tokens.shape),
        grad_tokens.reshape(tokens.shape),
        spec_sum(grad_proj, spec, count),
        vectors[4],
        vectors[5],
        spec_sum(grad_out, spec, count),
        vectors[3],
        spec_sum(grad_up, spec, count),
        vectors[8:].reshape(-1),
        spec_sum(grad_down, spec, count),
        vectors[0],
        vectors[6],
        vectors[7],
        vectors[1],
        vectors[2],
    )


def solution(mesh):
    return jax.shard_map(
        local,
        mesh=mesh,
        in_specs=(
            P("cube", "spec", None),
            P("cube", "spec", None),
            P("cube"),
        )
        + (P(),) * 13,
        out_specs=(
            P("cube", "spec", None),
            P("cube", "spec", None),
            P("cube", "spec"),
            P(),
            P(),
            P("cube", "spec"),
            P(),
            P("cube", "spec"),
            P(),
            P("cube", "spec"),
            P(),
            P(),
            P(),
            P(),
            P(),
        ),
        check_vma=False,
    )
```

time: 663 us -> 296 us (0.45)
  waiting for transfers between devices: 298 us -> 112 us
  matrix products: 154 us -> 0 us
  Pallas kernels: 0 us -> 94.5 us
  local copies, waits for them, and re-layouts: 76 us -> 22.6 us
  other arithmetic: 67.3 us -> 23 us
  blocking collectives: 41.6 us -> 0 us
  starting transfers between devices: 0.96 us -> 36.1 us
  between operations: 15.7 us -> 2.34 us
    reduce_scatter x5 -> x0, waiting for transfers between devices: 198 us -> none  [the longest x1 76.1 us: local(): lax.psum_scatter(matrices[2], 'cube', scatter_dimension=0, tiled=True)]
    dot_general x18 -> x0, matrix products: 154 us -> none  [the longest x4 26.9 us: left_dot(): lax.dot_general(left, right, (((0,), (0,)), ((), ())), preferred_element_...]
    ppermute x0 -> x42, waiting for transfers between devices: none -> 112 us  [the longest x10 42 us: tree_sum(): moved = lax.ppermute(send, 'cube', flip(cubes, 1 << bit))]
    pallas_call x0 -> x11, Pallas kernels: none -> 94.5 us  [the longest x1 30.2 us: middle_step(): pl.pallas_call(middle_kernel, out_shape=out_shape, grid_spec=pltpu.Prefet...]
    all_gather x2 -> x0, waiting for transfers between devices: 65.6 us -> none  [the longest x1 47.6 us: local(): lax.all_gather(key_part, 'spec', axis=1, tiled=True)]
    unnamed x85 -> x123, local copies, waits for them, and re-layouts: 62.3 us -> 14.8 us
    psum x1 -> x0, blocking collectives: 41.6 us -> none  [local(): lax.psum((grad_query_bias, grad_value_bias, grad_output_bias, grad_up_bia...]
    ppermute x0 -> x42, starting transfers between devices: none -> 36.1 us  [the longest x12 12.8 us: spec_sum(): lax.ppermute(mine(d).astype(BF), 'spec', flip(count, d))]
  transfers between devices with their start and end apart: 12 -> 42, of which waited for: 8 -> 19; matrix products, arithmetic and copies ran while one was open for 36% -> 11% of each run, Pallas kernels for 0% -> 20%
where the time goes in v1:
time: 296 us; the launch traced here: 290 us
  waiting for transfers between devices  112 us (38%)
  Pallas kernels  94.5 us (32%)
  starting transfers between devices  36.1 us (12%)
  other arithmetic  23 us (8%)
  local copies, waits for them, and re-layouts  22.6 us (8%)
    ppermute x10, waiting for transfers between devices, tree_sum(): moved = lax.ppermute(send, 'cube', flip(cubes, 1 << bit))  42 us
    ppermute x12, waiting for transfers between devices, spec_sum(): lax.ppermute(mine(d).astype(BF), 'spec', flip(count, d))  33.3 us
    pallas_call x1, Pallas kernels, middle_step(): pl.pallas_call(middle_kernel, out_shape=out_shape, grid_spec=pltpu.Prefet...  30.2 us
    pallas_call x4, Pallas kernels, backward_step(): pl.pallas_call(partial(backward_kernel, first, last), out_shape=outs, in_...  28.5 us
    ppermute x3, waiting for transfers between devices, local(): blocks.append(lax.ppermute(blocks[-1], 'spec', ring))  22.4 us
    pallas_call x4, Pallas kernels, forward_step(): pl.pallas_call(partial(forward_kernel, first, last), out_shape=outs, in_s...  21.6 us
    unnamed x123, local copies, waits for them, and re-layouts  14.8 us
    ppermute x12, starting transfers between devices, spec_sum(): lax.ppermute(mine(d).astype(BF), 'spec', flip(count, d))  12.8 us
  transfers between devices with their start and end apart: 42, of which 19 were waited for; matrix products, arithmetic and copies ran while one was open for 11% of the time, Pallas kernels for 20%

profile of v1, /device:TPU:0, one launch (start us, length us, event | category | flops | bytes accessed | tf_op | source)
XLA Modules:
  0.0 290.3 jit_solution(13664375970790981438)
XLA Ops:
  0.7 3.1 %collective-permute-start = (bf16[384,768]{1,0:T(8,128)(2,1)}, bf16[384,768]{1,0:T(8,128)(2,1)S(1)}, u32[]{:S(2)}, u32[]{:S(2)}) collective-permute-start(bf16[384,768]{1,0:T(8,128)(2,1)} %bitcast.9), channel_id=1, source_target_pairs={{0,1},{1,2},{2,3},{3,0},{4,5},{5,6},{6,7},{7,4},{8,9},{9,10},{10,1... | collective-permute-start | bytes 1769480 | tf_op jit(solution)/shard_map/ppermute | solution.py:605
  9.3 10.0 %collective-permute-done.refs_1_.refs_9_ = bf16[384,768]{1,0:T(8,128)(2,1)S(1)} collective-permute-done((bf16[384,768]{1,0:T(8,128)(2,1)}, bf16[384,768]{1,0:T(8,128)(2,1)S(1)}, u32[]{:S(2)}, u32[]{:S(2)}) %collective-permute-start) | collective-permute-done | bytes 589856 | tf_op jit(solution)/shard_map/ppermute | solution.py:605
  21.9 5.6 %attend_first.1 = (bf16[384,768]{1,0:T(8,128)(2,1)S(1)}, bf16[384,768]{1,0:T(8,128)(2,1)S(1)}, bf16[384,768]{1,0:T(8,128)(2,1)S(1)}, f32[8,768]{1,0:T(8,128)S(1)...) custom-call(s32[2]{0:T(128)S(1)} %pad_add_fusion.2.refs_0_, ...), custom_call_target="tpu_custom_call" | custom-call | flops 3170893824 | bytes 12582912 | tf_op jit(solution)/shard_map/attend_first/pallas_call | solution.py:146
  27.6 8.1 %collective-permute-done.1.refs_1_.refs_9_ = bf16[384,768]{1,0:T(8,128)(2,1)S(1)} collective-permute-done((bf16[384,768]{1,0:T(8,128)(2,1)S(1)}, bf16[384,768]{1,0:T(8,128)(2,1)S(1)}, u32[]{:S(2)}, u32[]{:S(2)}) %collective-permute-start.1) | collective-permute-done | bytes 589856 | tf_op jit(solution)/shard_map/ppermute | solution.py:605
  35.9 5.1 %attend_next.2 = (bf16[384,768]{1,0:T(8,128)(2,1)S(1)}, bf16[384,768]{1,0:T(8,128)(2,1)S(1)}, bf16[384,768]{1,0:T(8,128)(2,1)S(1)}, f32[8,768]{1,0:T(8,128)S(1)}...) custom-call(s32[2]{0:T(128)S(1)} %pad_add_fusion.4.refs_0_, bf16[384,768]{1,0:T(8,128)(2,1)S(1)} %collective-permute-done.refs_1_.refs_9_, ...), custom_call_target="tpu_custom_call" | custom-call | flops 2717908992 | bytes 12582912 | tf_op jit(solution)/shard_map/attend_next/pallas_call | solution.py:146
  41.9 5.1 %attend_next.3 = (bf16[384,768]{1,0:T(8,128)(2,1)S(1)}, bf16[384,768]{1,0:T(8,128)(2,1)S(1)}, bf16[384,768]{1,0:T(8,128)(2,1)S(1)}, f32[8,768]{1,0:T(8,128)S(1)}...) custom-call(s32[2]{0:T(128)S(1)} %get-tuple-element.177.refs_0_, ...), custom_call_target="tpu_custom_call" | custom-call | flops 2717908992 | bytes 12582912 | tf_op jit(solution)/shard_map/attend_next/pallas_call | solution.py:146
  46.9 4.3 %collective-permute-done.2.refs_1_.refs_9_ = bf16[384,768]{1,0:T(8,128)(2,1)S(1)} collective-permute-done((bf16[384,768]{1,0:T(8,128)(2,1)S(1)}, bf16[384,768]{1,0:T(8,128)(2,1)S(1)}, u32[]{:S(2)}, u32[]{:S(2)}) %collective-permute-start.2) | collective-permute-done | bytes 589856 | tf_op jit(solution)/shard_map/ppermute | solution.py:605
  51.2 5.9 %attend_last.1 = (bf16[384,768]{1,0:T(8,128)(2,1)S(1)}, bf16[384,768]{1,0:T(8,128)(2,1)S(1)}, bf16[384,768]{1,0:T(8,128)(2,1)S(1)}, f32[8,768]{1,0:T(8,128)S(1)}...) custom-call(s32[2]{0:T(128)S(1)} %get-tuple-element.176.refs_0_, bf16[384,768]{1,0:T(8,128)(2,1)S(1)} %collective-permute-done.2.refs_1_.refs_9_, ...), custom_call_target="tpu_custom_call" | custom-call | flops 2717908992 | bytes 12582912 | tf_op jit(solution)/shard_map/attend_last/pallas_call | solution.py:146
  58.0 30.2 %middle.1 = (bf16[384,768]{1,0:T(8,128)(2,1)}, bf16[1536,768]{1,0:T(8,128)(2,1)}, bf16[1536,768]{1,0:T(8,128)(2,1)}, bf16[384,3072]{1,0:T(8,128)(2,1)}, bf16[384...) custom-call(s32[8]{0:T(128)S(1)} %broadcast_xor_fusion.order_ref, ...), custom_call_target="tpu_custom_call" | custom-call | flops 12230590464 | bytes 31457280 | tf_op jit(solution)/shard_map/middle/pallas_call | solution.py:321
  95.4 7.5 %attend_back.4 = (bf16[384,1536]{1,0:T(8,128)(2,1)S(1)}, bf16[384,768]{1,0:T(8,128)(2,1)}, f32[8,768]{1,0:T(8,128)S(1)}, f32[768,384]{1,0:T(8,128)S(1)}) custom-call(s32[2]{0:T(128)S(1)} %pad_add_fusion.4.refs_0_, bf16[384,768]{1,0:T(8,128)(2,1)S(1)} %copy-done.39, bf16[768,384]{1,0:T(8,128)(2,1)S(1)} %get-tuple-element.71.refs_6_.refs_2_, ...), custom_call_target="tpu_custom_call" | custom-call | flops 5435817984 | bytes 16777216 | tf_op jit(solution)/shard_map/attend_back/pallas_call | solution.py:443
  103.1 6.7 %attend_back.5 = (bf16[384,1536]{1,0:T(8,128)(2,1)S(1)}, bf16[384,768]{1,0:T(8,128)(2,1)S(1)}, f32[8,768]{1,0:T(8,128)S(1)}, f32[768,384]{1,0:T(8,128)S(1)}) custom-call(s32[2]{0:T(128)S(1)} %copy-done.13, bf16[384,768]{1,0:T(8,128)(2,1)S(1)} %copy-done.40, bf16[768,384]{1,0:T(8,128)(2,1)S(1)} %get-tuple-element.71.refs_6_.refs_2_, ...), custom_call_target="tpu_custom_call" | custom-call | flops 5435817984 | bytes 16777216 | tf_op jit(solution)/shard_map/attend_back/pallas_call | solution.py:443
  110.7 6.7 %attend_back.6 = (bf16[384,1536]{1,0:T(8,128)(2,1)S(1)}, bf16[384,768]{1,0:T(8,128)(2,1)S(1)}, f32[8,768]{1,0:T(8,128)S(1)}, f32[768,384]{1,0:T(8,128)S(1)}) custom-call(s32[2]{0:T(128)S(1)} %copy-done.11, bf16[384,768]{1,0:T(8,128)(2,1)S(1)} %copy-done.40, bf16[768,384]{1,0:T(8,128)(2,1)S(1)} %get-tuple-element.71.refs_6_.refs_2_, ...), custom_call_target="tpu_custom_call" | custom-call | flops 5435817984 | bytes 16777216 | tf_op jit(solution)/shard_map/attend_back/pallas_call | solution.py:443
  118.3 7.7 %attend_back.7 = (bf16[384,1536]{1,0:T(8,128)(2,1)S(1)}, f32[384,768]{1,0:T(8,128)S(1)}, f32[8,768]{1,0:T(8,128)S(1)}, bf16[384,768]{1,0:T(8,128)(2,1)S(1)}) custom-call(s32[2]{0:T(128)S(1)} %copy-done.23, bf16[384,768]{1,0:T(8,128)(2,1)S(1)} %copy-done.40, bf16[768,384]{1,0:T(8,128)(2,1)S(1)} %get-tuple-element.71.refs_6_.refs_2_, ...), custom_call_target="tpu_custom_call" | custom-call | flops 5888802816 | bytes 16777216 | tf_op jit(solution)/shard_map/attend_back/pallas_call | solution.py:443
  126.0 11.1 %projection_grad.1 = (bf16[384,2304]{1,0:T(8,128)(2,1)S(1)}, bf16[384,2304]{1,0:T(8,128)(2,1)}) custom-call(bf16[768,768]{1,0:T(8,128)(2,1)S(1)} %fusion.1.refs_0_, bf16[384,768]{1,0:T(8,128)(2,1)S(1)} %get-tuple-element.107.refs_1_, bf16[384,768]{1,0:T(8,128)(2,1)S(1)} %copy-done.33, bf16[384,768]{1,0:T(8,128)(2,1)S(1)} %get-tuple-element.109.refs_3_, ...), custom_call_target="tpu_custom_call" | custom-call | flops 4076863488 | bytes 12582912 | tf_op jit(solution)/shard_map/projection_grad/pallas_call | solution.py:493
  151.5 2.4 collective-permute-done.25
  159.3 4.7 %collective-permute-done.26 = bf16[96,768]{1,0:T(8,128)(2,1)S(1)} collective-permute-done((bf16[96,768]{1,0:T(8,128)(2,1)S(1)}, bf16[96,768]{1,0:T(8,128)(2,1)S(1)}, u32[]{:S(2)}, u32[]{:S(2)}) %collective-permute-start.26) | collective-permute-done | bytes 147488 | tf_op jit(solution)/shard_map/ppermute | solution.py:544
  166.6 7.7 %collective-permute-done.4 = bf16[384,768]{1,0:T(8,128)(2,1)S(1)} collective-permute-done((bf16[384,768]{1,0:T(8,128)(2,1)S(1)}, bf16[384,768]{1,0:T(8,128)(2,1)S(1)}, u32[]{:S(2)}, u32[]{:S(2)}) %collective-permute-start.4) | collective-permute-done | bytes 589856 | tf_op jit(solution)/shard_map/ppermute | solution.py:740
  181.5 3.0 %add_convert_fusion.11 = (bf16[96,2304]{1,0:T(8,128)(2,1)}, bf16[96,2304]{1,0:T(8,128)(2,1)}, bf16[96,2304]{1,0:T(8,128)(2,1)}, bf16[96,2304]{1,0:T(8,128)(2,1)}) fusion(bf16[384,2304]{1,0:T(8,128)(2,1)} %collective-permute-done.6, bf16[384,2304]{1,0:T(8,128)(2,1)S(1)} %get-tuple-element.116), kind=kLoop, calls=%fused_computation.25 | loop fusion | flops 3538944 | bytes 5308416 | tf_op jit(solution)/shard_map/convert_element_type | solution.py:545
  186.7 10.5 %collective-permute-done.28 = bf16[96,192]{1,0:T(8,128)(2,1)S(1)} collective-permute-done((bf16[96,192]{1,0:T(8,128)(2,1)S(1)}, bf16[96,192]{1,0:T(8,128)(2,1)S(1)}, u32[]{:S(2)}, u32[]{:S(2)}) %collective-permute-start.28) | collective-permute-done | bytes 36896 | tf_op jit(solution)/shard_map/ppermute | solution.py:556
  199.4 3.9 %collective-permute-done.29 = bf16[96,192]{1,0:T(8,128)(2,1)S(1)} collective-permute-done((bf16[96,192]{1,0:T(8,128)(2,1)}, bf16[96,192]{1,0:T(8,128)(2,1)S(1)}, u32[]{:S(2)}, u32[]{:S(2)}) %collective-permute-start.29) | collective-permute-done | bytes 36896 | tf_op jit(solution)/shard_map/ppermute | solution.py:556
  207.2 3.1 %norm_back.1 = f32[384,768]{1,0:T(8,128)} custom-call(bf16[384,768]{1,0:T(8,128)(2,1)S(1)} %bitcast.13, f32[1,768]{1,0:T(1,128)S(1)} %reshape.123.refs_2_.gain_ref, f32[384,768]{1,0:T(8,128)S(1)} %copy-done.1, bf16[384,768]{1,0:T(8,128)(2,1)} %collective-permute-done.5.recv_ref, f32[384,768]{1,0:T(8,128)S(1)} %get-tuple-element.106.gmid_ref), custom_call_target="tpu_custom_call" | custom-call | flops 5898240 | bytes 2949120 | tf_op jit(solution)/shard_map/norm_back/pallas_call | solution.py:520
  211.5 6.8 %collective-permute-done.7 = bf16[96,2304]{1,0:T(8,128)(2,1)S(1)} collective-permute-done((bf16[96,2304]{1,0:T(8,128)(2,1)}, bf16[96,2304]{1,0:T(8,128)(2,1)S(1)}, u32[]{:S(2)}, u32[]{:S(2)}) %collective-permute-start.7) | collective-permute-done | bytes 442400 | tf_op jit(solution)/shard_map/ppermute | solution.py:544
  219.4 2.4 add_convert_fusion.1
  223.4 2.5 add_convert_fusion.3
  228.0 3.2 %collective-permute-start.13 = (bf16[96,576]{1,0:T(8,128)(2,1)S(1)}, bf16[96,576]{1,0:T(8,128)(2,1)S(1)}, u32[]{:S(2)}, u32[]{:S(2)}) collective-permute-start(bf16[96,576]{1,0:T(8,128)(2,1)S(1)} %get-tuple-element.168), channel_id=1, source_target_pairs={{0,3},{1,2},{2,1},{3,0},{4,7},{5,6},{6,5},{7,4},{8,11},{9,10},{10,... | collective-permute-start | bytes 331784 | tf_op jit(solution)/shard_map/ppermute | solution.py:556
  231.2 14.9 %collective-permute-done.37 = bf16[768,768]{1,0:T(8,128)(2,1)S(1)} collective-permute-done((bf16[768,768]{1,0:T(8,128)(2,1)S(1)}, bf16[768,768]{1,0:T(8,128)(2,1)S(1)}, u32[]{:S(2)}, u32[]{:S(2)}) %collective-permute-start.37) | collective-permute-done | bytes 1179680 | tf_op jit(solution)/shard_map/ppermute | solution.py:544
  247.4 7.4 %collective-permute-done.31 = bf16[192,3072]{1,0:T(8,128)(2,1)S(1)} collective-permute-done((bf16[192,3072]{1,0:T(8,128)(2,1)S(1)}, bf16[192,3072]{1,0:T(8,128)(2,1)S(1)}, u32[]{:S(2)}, u32[]{:S(2)}) %collective-permute-start.31) | collective-permute-done | bytes 1179680 | tf_op jit(solution)/shard_map/ppermute | solution.py:544
  256.4 5.8 %collective-permute-done.38 = bf16[384,768]{1,0:T(8,128)(2,1)S(1)} collective-permute-done((bf16[384,768]{1,0:T(8,128)(2,1)S(1)}, bf16[384,768]{1,0:T(8,128)(2,1)S(1)}, u32[]{:S(2)}, u32[]{:S(2)}) %collective-permute-start.38) | collective-permute-done | bytes 589856 | tf_op jit(solution)/shard_map/ppermute | solution.py:544
  263.9 3.2 %collective-permute-start.41 = (bf16[384,192]{1,0:T(8,128)(2,1)S(1)}, bf16[384,192]{1,0:T(8,128)(2,1)S(1)}, u32[]{:S(2)}, u32[]{:S(2)}) collective-permute-start(bf16[384,192]{1,0:T(8,128)(2,1)S(1)} %get-tuple-element.159), channel_id=1, source_target_pairs={{0,3},{1,2},{2,1},{3,0},{4,7},{5,6},{6,5},{7,4},{8,11},{9,10},{10,... | collective-permute-start | bytes 442376 | tf_op jit(solution)/shard_map/ppermute | solution.py:556
  268.6 3.5 %collective-permute-done.39 = bf16[384,192]{1,0:T(8,128)(2,1)S(1)} collective-permute-done((bf16[384,192]{1,0:T(8,128)(2,1)S(1)}, bf16[384,192]{1,0:T(8,128)(2,1)S(1)}, u32[]{:S(2)}, u32[]{:S(2)}) %collective-permute-start.39) | collective-permute-done | bytes 147488 | tf_op jit(solution)/shard_map/ppermute | solution.py:556
  272.8 9.8 %collective-permute-done.40 = bf16[384,192]{1,0:T(8,128)(2,1)S(1)} collective-permute-done((bf16[384,192]{1,0:T(8,128)(2,1)S(1)}, bf16[384,192]{1,0:T(8,128)(2,1)S(1)}, u32[]{:S(2)}, u32[]{:S(2)}) %collective-permute-start.40) | collective-permute-done | bytes 147488 | tf_op jit(solution)/shard_map/ppermute | solution.py:556
  283.6 5.6 %collective-permute-done.34 = bf16[96,768]{1,0:T(8,128)(2,1)S(1)} collective-permute-done((bf16[96,768]{1,0:T(8,128)(2,1)S(1)}, bf16[96,768]{1,0:T(8,128)(2,1)S(1)}, u32[]{:S(2)}, u32[]{:S(2)}) %collective-permute-start.34) | collective-permute-done | bytes 147488 | tf_op jit(solution)/shard_map/ppermute | solution.py:556
  (249 shorter events, 70.7 us)
Async XLA Ops:
  0.7 18.6 %collective-permute-start = (bf16[384,768]{1,0:T(8,128)(2,1)}, bf16[384,768]{1,0:T(8,128)(2,1)S(1)}, u32[]{:S(2)}, u32[]{:S(2)}) collective-permute-start(bf16[384,768]{1,0:T(8,128)(2,1)} %bitcast.9), channel_id=1, source_target_pairs={{0,1},{1,2},{2,3},{3,0},{4,5},{5,6},{6,7},{7,4},{8,9},{9,10},{10,1... | collective-permute-start | bytes 1769480 | tf_op jit(solution)/shard_map/ppermute | solution.py:605
  19.4 16.3 %collective-permute-start.1 = (bf16[384,768]{1,0:T(8,128)(2,1)S(1)}, bf16[384,768]{1,0:T(8,128)(2,1)S(1)}, u32[]{:S(2)}, u32[]{:S(2)}) collective-permute-start(bf16[384,768]{1,0:T(8,128)(2,1)S(1)} %collective-permute-done.refs_1_.refs_9_), channel_id=1, source_target_pairs={{0,1},{1,2},{2,3},{3,0},{4,5},{5,6},{6,7},{7,4},{8,9},{9,10},{10,1... | collective-permute-start | bytes 1769480 | tf_op jit(solution)/shard_map/ppermute | solution.py:605
  35.7 15.5 %collective-permute-start.2 = (bf16[384,768]{1,0:T(8,128)(2,1)S(1)}, bf16[384,768]{1,0:T(8,128)(2,1)S(1)}, u32[]{:S(2)}, u32[]{:S(2)}) collective-permute-start(bf16[384,768]{1,0:T(8,128)(2,1)S(1)} %collective-permute-done.1.refs_1_.refs_9_), channel_id=1, source_target_pairs={{0,1},{1,2},{2,3},{3,0},{4,5},{5,6},{6,7},{7,4},{8,9},{9,10},{10,1... | collective-permute-start | bytes 1769480 | tf_op jit(solution)/shard_map/ppermute | solution.py:605
  89.9 52.8 %collective-permute-start.24 = (bf16[384,768]{1,0:T(8,128)(2,1)}, bf16[384,768]{1,0:T(8,128)(2,1)}, u32[]{:S(2)}, u32[]{:S(2)}) collective-permute-start(bf16[384,768]{1,0:T(8,128)(2,1)} %get-tuple-element.122), channel_id=1, source_target_pairs={{0,4},{4,0},{8,12},{12,8},{16,20},{20,16},{24,28},{28,24},{1,5},{5... | collective-permute-start | bytes 1769480 | tf_op jit(solution)/shard_map/ppermute | solution.py:705
  102.9 43.9 %collective-permute-start.3 = (bf16[384,768]{1,0:T(8,128)(2,1)}, bf16[384,768]{1,0:T(8,128)(2,1)}, u32[]{:S(2)}, u32[]{:S(2)}) collective-permute-start(bf16[384,768]{1,0:T(8,128)(2,1)} %get-tuple-element.105), channel_id=1, source_target_pairs={{0,1},{1,2},{2,3},{3,0},{4,5},{5,6},{6,7},{7,4},{8,9},{9,10},{10,1... | collective-permute-start | bytes 1769480 | tf_op jit(solution)/shard_map/ppermute | solution.py:740
  137.1 42.2 %collective-permute-start.6 = (bf16[384,2304]{1,0:T(8,128)(2,1)}, bf16[384,2304]{1,0:T(8,128)(2,1)}, u32[]{:S(2)}, u32[]{:S(2)}) collective-permute-start(bf16[384,2304]{1,0:T(8,128)(2,1)} %get-tuple-element.117), channel_id=1, source_target_pairs={{0,4},{4,0},{8,12},{12,8},{16,20},{20,16},{24,28},{28,24},{1,5},{5... | collective-permute-start | bytes 5308424 | tf_op jit(solution)/shard_map/ppermute | solution.py:743
  144.0 9.9 %collective-permute-start.25 = (bf16[192,768]{1,0:T(8,128)(2,1)S(1)}, bf16[192,768]{1,0:T(8,128)(2,1)S(1)}, u32[]{:S(2)}, u32[]{:S(2)}) collective-permute-start(bf16[192,768]{1,0:T(8,128)(2,1)S(1)} %get-tuple-element.165), channel_id=1, source_target_pairs={{0,16},{4,20},{8,24},{12,28},{16,0},{20,4},{24,8},{28,12},{1,17},{... | collective-permute-start | bytes 884744 | tf_op jit(solution)/shard_map/ppermute | solution.py:544
  148.3 7.5 %collective-permute-start.17 = (f32[12,768]{1,0:T(8,128)S(1)}, f32[12,768]{1,0:T(8,128)S(1)}, u32[]{:S(2)}, u32[]{:S(2)}) collective-permute-start(f32[12,768]{1,0:T(8,128)S(1)} %pad_maximum_fusion), channel_id=1, source_target_pairs={{0,16},{4,20},{8,24},{12,28},{16,0},{20,4},{24,8},{28,12},{1,17},{... | collective-permute-start | bytes 110600 | tf_op jit(solution)/shard_map/ppermute | solution.py:567
  155.8 63.6 %collective-permute-start.36 = (bf16[1536,768]{1,0:T(8,128)(2,1)}, bf16[1536,768]{1,0:T(8,128)(2,1)}, u32[]{:S(2)}, u32[]{:S(2)}) collective-permute-start(bf16[1536,768]{1,0:T(8,128)(2,1)} %get-tuple-element.126), channel_id=1, source_target_pairs={{0,4},{4,0},{8,12},{12,8},{16,20},{20,16},{24,28},{28,24},{1,5},{5... | collective-permute-start | bytes 7077896 | tf_op jit(solution)/shard_map/ppermute | solution.py:703
  156.1 67.3 %collective-permute-start.30 = (bf16[384,3072]{1,0:T(8,128)(2,1)}, bf16[384,3072]{1,0:T(8,128)(2,1)}, u32[]{:S(2)}, u32[]{:S(2)}) collective-permute-start(bf16[384,3072]{1,0:T(8,128)(2,1)} %get-tuple-element.124), channel_id=1, source_target_pairs={{0,4},{4,0},{8,12},{12,8},{16,20},{20,16},{24,28},{28,24},{1,5},{5... | collective-permute-start | bytes 7077896 | tf_op jit(solution)/shard_map/ppermute | solution.py:704
  156.4 17.9 %collective-permute-start.4 = (bf16[384,768]{1,0:T(8,128)(2,1)S(1)}, bf16[384,768]{1,0:T(8,128)(2,1)S(1)}, u32[]{:S(2)}, u32[]{:S(2)}) collective-permute-start(bf16[384,768]{1,0:T(8,128)(2,1)S(1)} %add_convert_fusion.9), channel_id=1, source_target_pairs={{0,1},{1,2},{2,3},{3,0},{4,5},{5,6},{6,7},{7,4},{8,9},{9,10},{10,1... | collective-permute-start | bytes 1769480 | tf_op jit(solution)/shard_map/ppermute | solution.py:740
  164.0 11.1 %collective-permute-start.21 = (f32[12,768]{1,0:T(8,128)S(1)}, f32[12,768]{1,0:T(8,128)S(1)}, u32[]{:S(2)}, u32[]{:S(2)}) collective-permute-start(f32[12,768]{1,0:T(8,128)S(1)} %add_add_fusion.1), channel_id=1, source_target_pairs={{0,1},{1,0},{2,3},{3,2},{4,5},{5,4},{6,7},{7,6},{8,9},{9,8},{10,11... | collective-permute-start | bytes 110600 | tf_op jit(solution)/shard_map/ppermute | solution.py:570
  175.2 9.3 %collective-permute-start.23 = (f32[12,768]{1,0:T(8,128)S(1)}, f32[12,768]{1,0:T(8,128)S(1)}, u32[]{:S(2)}, u32[]{:S(2)}) collective-permute-start(f32[12,768]{1,0:T(8,128)S(1)} %add_add_fusion.1), channel_id=1, source_target_pairs={{0,3},{1,2},{2,1},{3,0},{4,7},{5,6},{6,5},{7,4},{8,11},{9,10},{10,... | collective-permute-start | bytes 110600 | tf_op jit(solution)/shard_map/ppermute | solution.py:570
  179.2 26.7 %collective-permute-start.5 = (bf16[384,768]{1,0:T(8,128)(2,1)}, bf16[384,768]{1,0:T(8,128)(2,1)}, u32[]{:S(2)}, u32[]{:S(2)}) collective-permute-start(bf16[384,768]{1,0:T(8,128)(2,1)} %add_convert_fusion.8), channel_id=1, source_target_pairs={{0,1},{1,2},{2,3},{3,0},{4,5},{5,6},{6,7},{7,4},{8,9},{9,10},{10,1... | collective-permute-start | bytes 1769480 | tf_op jit(solution)/shard_map/ppermute | solution.py:740
  184.5 12.6 %collective-permute-start.28 = (bf16[96,192]{1,0:T(8,128)(2,1)S(1)}, bf16[96,192]{1,0:T(8,128)(2,1)S(1)}, u32[]{:S(2)}, u32[]{:S(2)}) collective-permute-start(bf16[96,192]{1,0:T(8,128)(2,1)S(1)} %get-tuple-element.171), channel_id=1, source_target_pairs={{0,2},{1,3},{2,0},{3,1},{4,6},{5,7},{6,4},{7,5},{8,10},{9,11},{10,... | collective-permute-start | bytes 110600 | tf_op jit(solution)/shard_map/ppermute | solution.py:556
  185.6 24.7 %collective-permute-start.9 = (bf16[96,2304]{1,0:T(8,128)(2,1)}, bf16[96,2304]{1,0:T(8,128)(2,1)S(1)}, u32[]{:S(2)}, u32[]{:S(2)}) collective-permute-start(bf16[96,2304]{1,0:T(8,128)(2,1)} %get-tuple-element.155), channel_id=1, source_target_pairs={{0,16},{4,20},{8,24},{12,28},{16,0},{20,4},{24,8},{28,12},{1,17},{... | collective-permute-start | bytes 1327112 | tf_op jit(solution)/shard_map/ppermute | solution.py:544
  204.9 13.3 %collective-permute-start.7 = (bf16[96,2304]{1,0:T(8,128)(2,1)}, bf16[96,2304]{1,0:T(8,128)(2,1)S(1)}, u32[]{:S(2)}, u32[]{:S(2)}) collective-permute-start(bf16[96,2304]{1,0:T(8,128)(2,1)} %get-tuple-element.156), channel_id=1, source_target_pairs={{0,8},{4,12},{8,0},{12,4},{16,24},{20,28},{24,16},{28,20},{1,9},{5... | collective-permute-start | bytes 1327112 | tf_op jit(solution)/shard_map/ppermute | solution.py:544
  210.3 16.1 %collective-permute-start.10 = (bf16[48,2304]{1,0:T(8,128)(2,1)S(1)}, bf16[48,2304]{1,0:T(8,128)(2,1)S(1)}, u32[]{:S(2)}, u32[]{:S(2)}) collective-permute-start(bf16[48,2304]{1,0:T(8,128)(2,1)S(1)} %add_convert_fusion.16), channel_id=1, source_target_pairs={{0,8},{4,12},{8,0},{12,4},{16,24},{20,28},{24,16},{28,20},{1,9},{5... | collective-permute-start | bytes 663560 | tf_op jit(solution)/shard_map/ppermute | solution.py:544
  218.3 8.2 %collective-permute-start.8 = (bf16[48,2304]{1,0:T(8,128)(2,1)S(1)}, bf16[48,2304]{1,0:T(8,128)(2,1)S(1)}, u32[]{:S(2)}, u32[]{:S(2)}) collective-permute-start(bf16[48,2304]{1,0:T(8,128)(2,1)S(1)} %add_convert_fusion.18), channel_id=1, source_target_pairs={{0,16},{4,20},{8,24},{12,28},{16,0},{20,4},{24,8},{28,12},{1,17},{... | collective-permute-start | bytes 663560 | tf_op jit(solution)/shard_map/ppermute | solution.py:544
  221.8 24.3 %collective-permute-start.37 = (bf16[768,768]{1,0:T(8,128)(2,1)S(1)}, bf16[768,768]{1,0:T(8,128)(2,1)S(1)}, u32[]{:S(2)}, u32[]{:S(2)}) collective-permute-start(bf16[768,768]{1,0:T(8,128)(2,1)S(1)} %get-tuple-element.151), channel_id=1, source_target_pairs={{0,8},{4,12},{8,0},{12,4},{16,24},{20,28},{24,16},{28,20},{1,9},{5... | collective-permute-start | bytes 3538952 | tf_op jit(solution)/shard_map/ppermute | solution.py:544
  225.9 28.9 %collective-permute-start.31 = (bf16[192,3072]{1,0:T(8,128)(2,1)S(1)}, bf16[192,3072]{1,0:T(8,128)(2,1)S(1)}, u32[]{:S(2)}, u32[]{:S(2)}) collective-permute-start(bf16[192,3072]{1,0:T(8,128)(2,1)S(1)} %get-tuple-element.153), channel_id=1, source_target_pairs={{0,16},{4,20},{8,24},{12,28},{16,0},{20,4},{24,8},{28,12},{1,17},{... | collective-permute-start | bytes 3538952 | tf_op jit(solution)/shard_map/ppermute | solution.py:544
  226.8 28.8 %collective-permute-start.11 = (bf16[96,576]{1,0:T(8,128)(2,1)S(1)}, bf16[96,576]{1,0:T(8,128)(2,1)S(1)}, u32[]{:S(2)}, u32[]{:S(2)}) collective-permute-start(bf16[96,576]{1,0:T(8,128)(2,1)S(1)} %get-tuple-element.166), channel_id=1, source_target_pairs={{0,1},{1,0},{2,3},{3,2},{4,5},{5,4},{6,7},{7,6},{8,9},{9,8},{10,11... | collective-permute-start | bytes 331784 | tf_op jit(solution)/shard_map/ppermute | solution.py:556
  226.9 28.7 %collective-permute-start.12 = (bf16[96,576]{1,0:T(8,128)(2,1)S(1)}, bf16[96,576]{1,0:T(8,128)(2,1)S(1)}, u32[]{:S(2)}, u32[]{:S(2)}) collective-permute-start(bf16[96,576]{1,0:T(8,128)(2,1)S(1)} %get-tuple-element.167), channel_id=1, source_target_pairs={{0,2},{1,3},{2,0},{3,1},{4,6},{5,7},{6,4},{7,5},{8,10},{9,11},{10,... | collective-permute-start | bytes 331784 | tf_op jit(solution)/shard_map/ppermute | solution.py:556
  228.0 27.6 %collective-permute-start.13 = (bf16[96,576]{1,0:T(8,128)(2,1)S(1)}, bf16[96,576]{1,0:T(8,128)(2,1)S(1)}, u32[]{:S(2)}, u32[]{:S(2)}) collective-permute-start(bf16[96,576]{1,0:T(8,128)(2,1)S(1)} %get-tuple-element.168), channel_id=1, source_target_pairs={{0,3},{1,2},{2,1},{3,0},{4,7},{5,6},{6,5},{7,4},{8,11},{9,10},{10,... | collective-permute-start | bytes 331784 | tf_op jit(solution)/shard_map/ppermute | solution.py:556
  246.2 16.0 %collective-permute-start.38 = (bf16[384,768]{1,0:T(8,128)(2,1)S(1)}, bf16[384,768]{1,0:T(8,128)(2,1)S(1)}, u32[]{:S(2)}, u32[]{:S(2)}) collective-permute-start(bf16[384,768]{1,0:T(8,128)(2,1)S(1)} %add_convert_fusion.4), channel_id=1, source_target_pairs={{0,16},{4,20},{8,24},{12,28},{16,0},{20,4},{24,8},{28,12},{1,17},{... | collective-permute-start | bytes 1769480 | tf_op jit(solution)/shard_map/ppermute | solution.py:544
  254.9 12.2 %collective-permute-start.32 = (bf16[96,3072]{1,0:T(8,128)(2,1)S(1)}, bf16[96,3072]{1,0:T(8,128)(2,1)S(1)}, u32[]{:S(2)}, u32[]{:S(2)}) collective-permute-start(bf16[96,3072]{1,0:T(8,128)(2,1)S(1)} %add_convert_fusion.6), channel_id=1, source_target_pairs={{0,8},{4,12},{8,0},{12,4},{16,24},{20,28},{24,16},{28,20},{1,9},{5... | collective-permute-start | bytes 1769480 | tf_op jit(solution)/shard_map/ppermute | solution.py:544
  262.7 9.5 %collective-permute-start.39 = (bf16[384,192]{1,0:T(8,128)(2,1)S(1)}, bf16[384,192]{1,0:T(8,128)(2,1)S(1)}, u32[]{:S(2)}, u32[]{:S(2)}) collective-permute-start(bf16[384,192]{1,0:T(8,128)(2,1)S(1)} %get-tuple-element.158), channel_id=1, source_target_pairs={{0,1},{1,0},{2,3},{3,2},{4,5},{5,4},{6,7},{7,6},{8,9},{9,8},{10,11... | collective-permute-start | bytes 442376 | tf_op jit(solution)/shard_map/ppermute | solution.py:556
  262.8 19.8 %collective-permute-start.40 = (bf16[384,192]{1,0:T(8,128)(2,1)S(1)}, bf16[384,192]{1,0:T(8,128)(2,1)S(1)}, u32[]{:S(2)}, u32[]{:S(2)}) collective-permute-start(bf16[384,192]{1,0:T(8,128)(2,1)S(1)} %get-tuple-element.160), channel_id=1, source_target_pairs={{0,2},{1,3},{2,0},{3,1},{4,6},{5,7},{6,4},{7,5},{8,10},{9,11},{10,... | collective-permute-start | bytes 442376 | tf_op jit(solution)/shard_map/ppermute | solution.py:556
  263.9 18.7 %collective-permute-start.41 = (bf16[384,192]{1,0:T(8,128)(2,1)S(1)}, bf16[384,192]{1,0:T(8,128)(2,1)S(1)}, u32[]{:S(2)}, u32[]{:S(2)}) collective-permute-start(bf16[384,192]{1,0:T(8,128)(2,1)S(1)} %get-tuple-element.159), channel_id=1, source_target_pairs={{0,3},{1,2},{2,1},{3,0},{4,7},{5,6},{6,5},{7,4},{8,11},{9,10},{10,... | collective-permute-start | bytes 442376 | tf_op jit(solution)/shard_map/ppermute | solution.py:556
  267.4 16.2 %collective-permute-start.33 = (bf16[96,768]{1,0:T(8,128)(2,1)S(1)}, bf16[96,768]{1,0:T(8,128)(2,1)S(1)}, u32[]{:S(2)}, u32[]{:S(2)}) collective-permute-start(bf16[96,768]{1,0:T(8,128)(2,1)S(1)} %get-tuple-element.161), channel_id=1, source_target_pairs={{0,1},{1,0},{2,3},{3,2},{4,5},{5,4},{6,7},{7,6},{8,9},{9,8},{10,11... | collective-permute-start | bytes 442376 | tf_op jit(solution)/shard_map/ppermute | solution.py:556
  267.5 21.8 %collective-permute-start.34 = (bf16[96,768]{1,0:T(8,128)(2,1)S(1)}, bf16[96,768]{1,0:T(8,128)(2,1)S(1)}, u32[]{:S(2)}, u32[]{:S(2)}) collective-permute-start(bf16[96,768]{1,0:T(8,128)(2,1)S(1)} %get-tuple-element.163), channel_id=1, source_target_pairs={{0,2},{1,3},{2,0},{3,1},{4,6},{5,7},{6,4},{7,5},{8,10},{9,11},{10,... | collective-permute-start | bytes 442376 | tf_op jit(solution)/shard_map/ppermute | solution.py:556
  272.2 17.1 %collective-permute-start.35 = (bf16[96,768]{1,0:T(8,128)(2,1)S(1)}, bf16[96,768]{1,0:T(8,128)(2,1)S(1)}, u32[]{:S(2)}, u32[]{:S(2)}) collective-permute-start(bf16[96,768]{1,0:T(8,128)(2,1)S(1)} %get-tuple-element.162), channel_id=1, source_target_pairs={{0,3},{1,2},{2,1},{3,0},{4,7},{5,6},{6,5},{7,4},{8,11},{9,10},{10,... | collective-permute-start | bytes 442376 | tf_op jit(solution)/shard_map/ppermute | solution.py:556
  (71 other events, 693.8 us)
